TPU v7x, 128 devices: a whole 4x4x4 slice. The times are simulated.
128 devices in a mesh: row: 8 (over x, core), col: 16 (over y, z).
Axes of the slice: x: 4, y: 4, z: 4, core: 2. Of those that a mesh axis runs over, the one named last changes fastest.
Arguments:
- eta_pairs: bfloat16 [12288, 12288], P('row', 'col'), may hold values from -6 to 6
- gamma_pairs: bfloat16 [12288, 12288], P('row', 'col'), may hold values from -0.0546875 to 0.0546875
- pair_first: int32 [12288], P('row'), may hold values from 0 to 239
- pair_second: int32 [12288], P('row'), may hold values from 0 to 239
- occupancy: float32 [240], replicated, may hold values from 0 to 1
- gamma_recoupled: bfloat16 [128, 1536, 1536], P(('row', 'col')), may hold values from -0.15625 to 0.15625
- ph_factor: float32 [128, 1536], P(('row', 'col')), may hold values from -1 to 1
- tile_source: int32 [128, 144], P(('row', 'col')), may hold values from 0 to 71, as said below
- tile_owner: int32 [128, 144], P(('row', 'col')), may hold values from 0 to 127, as said below
- tile_place: int32 [128, 144], P(('row', 'col')), may hold values from 0 to 143
- sixj_weight: bfloat16 [128, 144], P(('row', 'col')), may hold values from -1 to 1
- live_count: int32 [128], P(('row', 'col')), may hold values from 72 to 144, as said below
Outputs:
- panel_update: bfloat16 [2048, 12288], P('col', 'row')
- recoupled_update: bfloat16 [12288, 12288], P('row', 'col')
Inputs may be any that keep to these rules, and one draw needn't show every extreme that they name: `tile_source`: in each row the first 72 entries name every tile of the block once. `tile_owner`: in each row no channel is named by more than 2 entries; one channel is named exactly 2 times within the first 72 entries of every row. `live_count`: some block has 144 live slots and another 72.
All inputs are finite; a program needn't handle non-finite values.
Results may differ from a plain program's by a relative error of at most 0.019.
Values may be sent and summed in bfloat16 or wider, within the bound.
No kernel may reach another device: no remote copies, remote signals or barrier semaphores. Data moves between devices by JAX's collectives and lax.ppermute only.
A program may use at most 128 MiB of HBM per device.

v0:
```python
import jax
import jax.numpy as jnp
from jax import lax
from jax.sharding import PartitionSpec as P

TILE = 128
PH_STATES = 1536
PANEL_DEV = 128


def orbit_lookup(pair_ids, occupancy):
    orbit_ids = jnp.arange(occupancy.shape[0], dtype=jnp.int32)
    return jnp.sum(
        jnp.where(pair_ids[:, None] == orbit_ids[None, :], occupancy[None, :], 0.0), axis=1
    )


def panel_part(eta_pairs, gamma_pairs, pair_first, pair_second, occupancy):
    factor = 1.0 - orbit_lookup(pair_first, occupancy) - orbit_lookup(pair_second, occupancy)
    panel_width = PANEL_DEV
    gamma_cols = (
        (factor[:, None] * gamma_pairs[:, :panel_width].astype(jnp.float32)).astype(jnp.bfloat16).T
    )
    eta_cols = (
        (factor[:, None] * eta_pairs[:, :panel_width].astype(jnp.float32)).astype(jnp.bfloat16).T
    )
    gamma_whole, eta_whole = (
        lax.all_gather(gamma_cols, "row", axis=1, tiled=True),
        lax.all_gather(eta_cols, "row", axis=1, tiled=True),
    )
    gamma_panel, eta_panel = (
        lax.all_to_all(gamma_whole, "col", split_axis=1, concat_axis=0, tiled=True),
        lax.all_to_all(eta_whole, "col", split_axis=1, concat_axis=0, tiled=True),
    )
    contract = (((1,), (1,)), ((), ()))
    leading = lax.dot_general(gamma_panel, eta_pairs, contract, preferred_element_type=jnp.float32)
    trailing = lax.dot_general(eta_panel, gamma_pairs, contract, preferred_element_type=jnp.float32)
    return lax.psum_scatter(
        (leading - trailing).astype(jnp.bfloat16), "col", scatter_dimension=0, tiled=True
    )


def deliver(sent_tiles, place_code):
    moved_tiles, moved_codes = (
        lax.all_to_all(sent_tiles, ("row", "col"), split_axis=0, concat_axis=0, tiled=True),
        lax.all_to_all(place_code, ("row", "col"), split_axis=0, concat_axis=0, tiled=True),
    )
    return (moved_tiles, moved_codes)


def collect(answer_tiles):
    return lax.all_to_all(answer_tiles, ("row", "col"), split_axis=0, concat_axis=0, tiled=True)


def recoupled_part(
    eta_pairs,
    gamma_recoupled,
    ph_factor,
    tile_source,
    tile_owner,
    tile_place,
    sixj_weight,
    live_count,
):
    n_row = lax.axis_size("row")
    n_col = lax.axis_size("col")
    blocks = n_row * n_col
    slot_total = tile_source.shape[1]
    capacity = max(2, (slot_total + blocks - 1) // blocks)
    row_tiles = eta_pairs.shape[0] // TILE
    col_tiles = eta_pairs.shape[1] // TILE
    block_tiles = row_tiles * col_tiles
    ph_tiles = PH_STATES // TILE
    tile_area = TILE * TILE
    eta_tiles = (
        eta_pairs.reshape(row_tiles, TILE, col_tiles, TILE)
        .transpose(0, 2, 1, 3)
        .reshape(block_tiles, tile_area)
    )
    sources = tile_source[0]
    owners = tile_owner[0]
    places = tile_place[0]
    weights = sixj_weight[0].astype(jnp.float32)
    slot_ids = jnp.arange(slot_total, dtype=jnp.int32)
    is_live = slot_ids < live_count[0]
    same_owner = (
        (owners[:, None] == owners[None, :])
        & is_live[None, :]
        & (slot_ids[None, :] < slot_ids[:, None])
    )
    slot_rank = jnp.sum(same_owner.astype(jnp.int32), axis=1)
    buffer_ids = jnp.arange(blocks * capacity, dtype=jnp.int32)
    slot_hit = (
        ((owners * capacity + slot_rank)[:, None] == buffer_ids[None, :]) & is_live[:, None]
    ).astype(jnp.float32)
    tile_ids = jnp.arange(block_tiles, dtype=jnp.int32)
    source_hit = (sources[:, None] == tile_ids[None, :]).astype(jnp.float32) * weights[:, None]
    highest = lax.Precision.HIGHEST
    lead_dims = (((0,), (0,)), ((), ()))
    outward = lax.dot_general(slot_hit, source_hit, lead_dims, precision=highest).astype(
        jnp.bfloat16
    )
    sent_tiles = jnp.dot(outward, eta_tiles, preferred_element_type=jnp.float32).astype(
        jnp.bfloat16
    )
    place_code = (
        lax.dot_general(slot_hit, places.astype(jnp.float32) + 1.0, lead_dims, precision=highest)
        - 1.0
    )
    place_code = place_code.astype(jnp.bfloat16)
    received, codes = deliver(
        sent_tiles.reshape(blocks, capacity, tile_area), place_code.reshape(blocks, capacity)
    )
    received = received.reshape(blocks * capacity, tile_area)
    codes = codes.reshape(blocks * capacity).astype(jnp.float32)
    positions = jnp.arange(ph_tiles * ph_tiles, dtype=jnp.float32)
    assemble = (positions[:, None] == codes[None, :]).astype(jnp.bfloat16)
    eta_ph = jnp.dot(assemble, received, preferred_element_type=jnp.float32).astype(jnp.bfloat16)
    eta_ph = (
        eta_ph.reshape(ph_tiles, ph_tiles, TILE, TILE)
        .transpose(0, 2, 1, 3)
        .reshape(PH_STATES, PH_STATES)
    )
    gamma_ph = gamma_recoupled[0]
    scale = ph_factor[0]
    gamma_scaled = (scale[:, None] * gamma_ph.astype(jnp.float32)).astype(jnp.bfloat16)
    eta_scaled = (scale[:, None] * eta_ph.astype(jnp.float32)).astype(jnp.bfloat16)
    product = jnp.dot(eta_ph, gamma_scaled, preferred_element_type=jnp.float32)
    product = (product - jnp.dot(gamma_ph, eta_scaled, preferred_element_type=jnp.float32)).astype(
        jnp.bfloat16
    )
    product_tiles = (
        product.reshape(ph_tiles, TILE, ph_tiles, TILE)
        .transpose(0, 2, 1, 3)
        .reshape(ph_tiles * ph_tiles, tile_area)
    )
    answer = lax.dot_general(
        assemble, product_tiles, lead_dims, preferred_element_type=jnp.float32
    ).astype(jnp.bfloat16)
    returned = collect(answer.reshape(blocks, capacity, tile_area)).reshape(
        blocks * capacity, tile_area
    )
    inward = lax.dot_general(source_hit, slot_hit, lead_dims, precision=highest).astype(
        jnp.bfloat16
    )
    update = jnp.dot(inward, returned, preferred_element_type=jnp.float32).astype(jnp.bfloat16)
    return (
        update.reshape(row_tiles, col_tiles, TILE, TILE)
        .transpose(0, 2, 1, 3)
        .reshape(eta_pairs.shape)
    )


def local(
    eta_pairs,
    gamma_pairs,
    pair_first,
    pair_second,
    occupancy,
    gamma_recoupled,
    ph_factor,
    tile_source,
    tile_owner,
    tile_place,
    sixj_weight,
    live_count,
):
    panel_update = panel_part(eta_pairs, gamma_pairs, pair_first, pair_second, occupancy)
    recoupled_update = recoupled_part(
        eta_pairs,
        gamma_recoupled,
        ph_factor,
        tile_source,
        tile_owner,
        tile_place,
        sixj_weight,
        live_count,
    )
    return (panel_update, recoupled_update)


def solution(mesh):
    in_specs = (
        P("row", "col"),
        P("row", "col"),
        P("row"),
        P("row"),
        P(),
        P(("row", "col"), None, None),
        P(("row", "col"), None),
        P(("row", "col"), None),
        P(("row", "col"), None),
        P(("row", "col"), None),
        P(("row", "col"), None),
        P(("row", "col")),
    )
    out_specs = (P("col", "row"), P("row", "col"))
    return jax.shard_map(local, mesh=mesh, in_specs=in_specs, out_specs=out_specs, check_vma=False)
```

profile of v0, /device:TPU:8, one launch (start us, length us, event | category | flops | bytes accessed | tf_op | source)
XLA Modules:
  0.0 508.7 jit_solution(10013048364006905309)
XLA Ops:
  7.8 0.9 convert_reduce_fusion
  8.8 0.7 multiply_add_fusion
  9.5 0.9 fusion.21
  10.4 0.8 all_to_all.52
  11.2 10.4 %all-to-all-start.2 = ((bf16[128,1,2]{2,1,0:T(2,128)(2,1)}), bf16[128,1,2]{2,1,0:T(2,128)(2,1)S(1)}, u32[]{:S(2)}, u32[]{:S(2)}) async-start(bf16[128,1,2]{2,1,0:T(2,128)(2,1)} %all_to_all.52), calls=%async_computation.3 | async-start | bytes 131072 | tf_op jit(solution)/shard_map/all_to_all | solution.py:46
  21.6 0.7 convert_element_type.114
  22.3 4.8 reshape.110
  27.2 0.7 copy.39
  27.8 0.0 copy-done.5
  27.8 0.4 convolution_convert_fusion.4
  28.2 0.0 copy-start.1
  28.2 0.0 copy-start.2
  28.2 0.0 copy-start.4
  28.2 5.7 %convolution_convert_fusion = bf16[256,16384]{1,0:T(8,128)(2,1)} fusion(bf16[256,72]{0,1:T(8,128)(2,1)S(1)} %convolution_convert_fusion.4, bf16[9,8,128,128]{3,2,1,0:T(8,128)(2,1)S(1)} %bitcast.86), kind=kOutput, calls=%fused_computation | convolution fusion | flops 608174080 | bytes 10784768 | tf_op jit(solution)/shard_map/dot_general | solution.py:103
  33.9 0.0 copy-done.1
  33.9 0.0 copy-done.2
  33.9 0.0 copy-done.4
  33.9 0.5 select_reduce_fusion.1
  34.4 14.1 %reshape.112 = bf16[128,2,16384]{2,1,0:T(2,128)(2,1)} reshape(bf16[256,16384]{1,0:T(8,128)(2,1)} %convolution_convert_fusion) | data formatting | bytes 16777216 | tf_op jit(solution)/shard_map/reshape | solution.py:112
  48.5 0.0 all-to-all-done.2
  48.5 10.2 %all-to-all-start.3 = ((bf16[128,2,16384]{2,1,0:T(2,128)(2,1)}), bf16[128,2,16384]{2,1,0:T(2,128)(2,1)}, u32[]{:S(2)}, u32[]{:S(2)}) async-start(bf16[128,2,16384]{2,1,0:T(2,128)(2,1)} %reshape.112), calls=%async_computation.4 | async-start | bytes 16777216 | tf_op jit(solution)/shard_map/all_to_all | solution.py:45
  58.7 0.0 all-gather.3.cloned.1.call-start
  58.8 2.3 fusion.17
  61.1 0.0 all-gather.3.cloned.1.call-update
  61.1 0.0 all-gather.5.cloned.1.call-start
  61.1 0.7 all-gather.5.cloned.1.call-update
  61.8 55.0 %all-gather.3.cloned.1.call-done = bf16[128,12288]{0,1:T(8,128)(2,1)} async-done(((bf16[128,1536]{0,1:T(8,128)(2,1)}), bf16[128,12288]{0,1:T(8,128)(2,1)}) %all-gather.3.cloned.1.call-update) | async-done | bytes 3145744 | tf_op jit(solution)/shard_map/all_gather | solution.py:28
  116.8 68.2 %all-to-all-done.3 = bf16[128,2,16384]{2,1,0:T(2,128)(2,1)} async-done(((bf16[128,2,16384]{2,1,0:T(2,128)(2,1)}), bf16[128,2,16384]{2,1,0:T(2,128)(2,1)}, u32[]{:S(2)}, u32[]{:S(2)}) %all-to-all-start.3) | async-done | bytes 8388640 | tf_op jit(solution)/shard_map/all_to_all | solution.py:45
  185.0 8.4 %all-to-all-start = ((bf16[128,16,768]{0,2,1:T(8,128)(2,1)}), bf16[128,16,768]{0,2,1:T(8,128)(2,1)S(1)}, u32[]{:S(2)}, u32[]{:S(2)}) async-start(bf16[128,16,768]{0,2,1:T(8,128)(2,1)} %bitcast.91), calls=%async_computation | async-start | bytes 6291456 | tf_op jit(solution)/shard_map/all_to_all | solution.py:32
  193.4 0.0 all-gather.5.cloned.1.call-done
  193.4 36.6 %all-to-all-done = bf16[128,16,768]{0,2,1:T(8,128)(2,1)S(1)} async-done(((bf16[128,16,768]{0,2,1:T(8,128)(2,1)}), bf16[128,16,768]{0,2,1:T(8,128)(2,1)S(1)}, u32[]{:S(2)}, u32[]{:S(2)}) %all-to-all-start) | async-done | bytes 3145760 | tf_op jit(solution)/shard_map/all_to_all | solution.py:32
  230.0 8.1 %all-to-all-start.1 = ((bf16[128,16,768]{0,2,1:T(8,128)(2,1)}), bf16[128,16,768]{0,2,1:T(8,128)(2,1)}, u32[]{:S(2)}, u32[]{:S(2)}) async-start(bf16[128,16,768]{0,2,1:T(8,128)(2,1)} %bitcast.90), calls=%async_computation.1 | async-start | bytes 6291456 | tf_op jit(solution)/shard_map/all_to_all | solution.py:33
  238.1 0.2 reduce-scatter.2.cloned.1.call-start
  238.3 0.0 copy-done.3
  238.4 0.2 convert_reduce_fusion.1
  238.5 0.1 reshape.123
  238.7 13.1 %reshape.113 = bf16[256,16384]{1,0:T(8,128)(2,1)} reshape(bf16[128,2,16384]{2,1,0:T(2,128)(2,1)} %all-to-all-done.3) | data formatting | bytes 16777216 | tf_op jit(solution)/shard_map/reshape | solution.py:114
  251.8 4.8 fusion.14
  256.6 1.4 copy.46
  258.0 0.0 copy-start
  258.0 7.1 %multiply_convert_fusion = bf16[12,128,12,128]{3,2,1,0:T(8,128)(2,1)} fusion(f32[12,128]{1,0:T(8,128)S(1)} %bitcast.95, bf16[12,12,128,128]{3,2,1,0:T(8,128)(2,1)S(1)} %bitcast.77), kind=kLoop, calls=%fused_computation.4 | loop fusion | flops 7077888 | bytes 9443328 | tf_op jit(solution)/shard_map/convert_element_type | solution.py:127
  265.1 0.0 copy-done
  265.1 2.8 copy.36
  267.9 10.1 %fusion.47 = f32[2048,1536]{1,0:T(8,128)} fusion(bf16[2048,768]{1,0:T(8,128)(2,1)} %bitcast.93, bf16[1536,768]{1,0:T(8,128)(2,1)} %param.12), kind=kOutput, calls=%fused_computation.70 | convolution fusion | flops 4831838208 | bytes 18087936 | tf_op jit(solution)/shard_map/dot_general | solution.py:36
  278.0 0.0 all-to-all-done.1
  278.0 3.2 copy.37
  281.2 10.5 %subtract_convert_fusion = bf16[2048,1536]{1,0:T(8,128)(2,1)} fusion(f32[2048,1536]{1,0:T(8,128)} %fusion.47, bf16[2048,768]{1,0:T(8,128)(2,1)S(1)} %bitcast.92, bf16[1536,768]{1,0:T(8,128)(2,1)} %param.13), kind=kOutput, calls=%fused_computation.5 | convolution fusion | flops 4838129664 | bytes 24379392 | tf_op jit(solution)/shard_map/dot_general | solution.py:37
  291.6 0.0 reduce-scatter.2.cloned.1.call-update
  291.7 0.0 slice-start.1
  291.7 13.7 %fusion.5 = f32[1536,1536]{0,1:T(8,128)} fusion(bf16[192,8,12,128]{3,2,1,0:T(8,128)(2,1)} %bitcast.88, bf16[1,1536,1536]{2,1,0:T(8,128)(2,1)} %param.17), kind=kOutput, calls=%fused_computation.12 | convolution fusion | flops 7247757312 | bytes 18874368 | tf_op jit(solution)/shard_map/dot_general | solution.py:129
  305.4 3.7 copy.40
  309.0 12.9 %fusion = bf16[1536,1536]{1,0:T(8,128)(2,1)} fusion(f32[1536,1536]{0,1:T(8,128)} %fusion.5, bf16[1,1536,1536]{2,1,0:T(8,128)(2,1)} %param.17, bf16[192,8,12,128]{3,2,1,0:T(8,128)(2,1)S(1)} %bitcast.89, f32[1536]{0:T(1024)S(1)} %reduce.1), kind=kOutput, calls=%fused_computation.7 | convolution fusion | flops 7259553792 | bytes 23599104 | tf_op jit(solution)/shard_map/dot_general | solution.py:128
  321.9 9.5 %reshape.116 = bf16[12,128,12,128]{3,2,1,0:T(8,128)(2,1)} reshape(bf16[1536,1536]{1,0:T(8,128)(2,1)} %fusion) | data formatting | bytes 9437184 | tf_op jit(solution)/shard_map/reshape | solution.py:133
  331.4 4.2 copy.42
  335.6 7.3 %convolution_convert_fusion.1 = bf16[256,16384]{1,0:T(8,128)(2,1)} fusion(bf16[18,8,128,128]{3,2,1,0:T(8,128)(2,1)S(1)} %bitcast.82, f32[256]{0:T(256)S(1)} %reshape.123), kind=kOutput, calls=%fused_computation.1 | convolution fusion | flops 1212190720 | bytes 13108224 | tf_op jit(solution)/shard_map/dot_general | solution.py:137
  342.9 14.2 %reshape.118 = bf16[128,2,16384]{2,1,0:T(2,128)(2,1)} reshape(bf16[256,16384]{1,0:T(8,128)(2,1)} %convolution_convert_fusion.1) | data formatting | bytes 16777216 | tf_op jit(solution)/shard_map/reshape | solution.py:140
  357.0 12.7 %all-to-all-start.4 = ((bf16[128,2,16384]{2,1,0:T(2,128)(2,1)}), bf16[128,2,16384]{2,1,0:T(2,128)(2,1)}, u32[]{:S(2)}, u32[]{:S(2)}) async-start(bf16[128,2,16384]{2,1,0:T(2,128)(2,1)} %reshape.118), calls=%async_computation.5 | async-start | bytes 16777216 | tf_op jit(solution)/shard_map/all_to_all | solution.py:52
  369.8 0.4 convolution_convert_fusion.5
  370.1 109.2 %all-to-all-done.4 = bf16[128,2,16384]{2,1,0:T(2,128)(2,1)} async-done(((bf16[128,2,16384]{2,1,0:T(2,128)(2,1)}), bf16[128,2,16384]{2,1,0:T(2,128)(2,1)}, u32[]{:S(2)}, u32[]{:S(2)}) %all-to-all-start.4) | async-done | bytes 8388640 | tf_op jit(solution)/shard_map/all_to_all | solution.py:52
  479.3 13.1 %reshape.119 = bf16[256,16384]{1,0:T(8,128)(2,1)} reshape(bf16[128,2,16384]{2,1,0:T(2,128)(2,1)} %all-to-all-done.4) | data formatting | bytes 16777216 | tf_op jit(solution)/shard_map/reshape | solution.py:140
  492.4 5.0 fusion.15
  497.3 0.7 copy.50
  498.0 1.8 copy.43
  499.8 2.0 copy.70
  (11 shorter events, 0.1 us)
Async XLA Ops:
  11.2 37.3 %all-to-all-start.2 = ((bf16[128,1,2]{2,1,0:T(2,128)(2,1)}), bf16[128,1,2]{2,1,0:T(2,128)(2,1)S(1)}, u32[]{:S(2)}, u32[]{:S(2)}) async-start(bf16[128,1,2]{2,1,0:T(2,128)(2,1)} %all_to_all.52), calls=%async_computation.3 | async-start | bytes 131072 | tf_op jit(solution)/shard_map/all_to_all | solution.py:46
  22.3 5.5 %copy-start.5 = (s32[1,144]{1,0:T(1,128)S(1)}, s32[1,144]{1,0:T(1,128)}, u32[]{:S(2)}) copy-start(s32[1,144]{1,0:T(1,128)} %param.19) | copy-start | bytes 1732
  28.2 5.7 %copy-start.1 = (s32[1536]{0:T(1024)S(1)}, s32[1536]{0:T(1024)}, u32[]{:S(2)}) copy-start(s32[1536]{0:T(1024)} %param.14) | copy-start | bytes 18436
  28.2 5.7 %copy-start.2 = (s32[1536]{0:T(1024)S(1)}, s32[1536]{0:T(1024)}, u32[]{:S(2)}) copy-start(s32[1536]{0:T(1024)} %param.15) | copy-start | bytes 18436
  28.2 5.7 %copy-start.4 = (f32[240]{0:T(256)S(1)}, f32[240]{0:T(256)}, u32[]{:S(2)}) copy-start(f32[240]{0:T(256)} %param.16) | copy-start | bytes 2884
  48.5 136.5 %all-to-all-start.3 = ((bf16[128,2,16384]{2,1,0:T(2,128)(2,1)}), bf16[128,2,16384]{2,1,0:T(2,128)(2,1)}, u32[]{:S(2)}, u32[]{:S(2)}) async-start(bf16[128,2,16384]{2,1,0:T(2,128)(2,1)} %reshape.112), calls=%async_computation.4 | async-start | bytes 16777216 | tf_op jit(solution)/shard_map/all_to_all | solution.py:45
  58.7 58.1 %all-gather.3.cloned.1.call-start = ((), (), s32[]{:S(2)}) async-start(), calls=%async_computation.6 | async-start | bytes 3538944 | tf_op jit(solution)/shard_map/all_gather | solution.py:28
  61.1 132.3 %all-gather.5.cloned.1.call-start = ((), (), s32[]{:S(2)}) async-start(), calls=%async_computation.7 | async-start | bytes 3538944 | tf_op jit(solution)/shard_map/all_gather | solution.py:29
  185.0 45.0 %all-to-all-start = ((bf16[128,16,768]{0,2,1:T(8,128)(2,1)}), bf16[128,16,768]{0,2,1:T(8,128)(2,1)S(1)}, u32[]{:S(2)}, u32[]{:S(2)}) async-start(bf16[128,16,768]{0,2,1:T(8,128)(2,1)} %bitcast.91), calls=%async_computation | async-start | bytes 6291456 | tf_op jit(solution)/shard_map/all_to_all | solution.py:32
  193.4 44.9 %copy-start.3 = (f32[1,1536]{1,0:T(1,128)S(1)}, f32[1,1536]{1,0:T(1,128)}, u32[]{:S(2)}) copy-start(f32[1,1536]{1,0:T(1,128)} %param.18) | copy-start | bytes 18436
  230.0 48.0 %all-to-all-start.1 = ((bf16[128,16,768]{0,2,1:T(8,128)(2,1)}), bf16[128,16,768]{0,2,1:T(8,128)(2,1)}, u32[]{:S(2)}, u32[]{:S(2)}) async-start(bf16[128,16,768]{0,2,1:T(8,128)(2,1)} %bitcast.90), calls=%async_computation.1 | async-start | bytes 6291456 | tf_op jit(solution)/shard_map/all_to_all | solution.py:33
  238.1 263.7 %reduce-scatter.2.cloned.1.call-start = ((), (), s32[]{:S(2)}) async-start(), calls=%async_computation.8 | async-start | bytes 6684672 | tf_op jit(solution)/shard_map/reduce_scatter | solution.py:38
  258.0 7.1 %copy-start = (bf16[18,8,128,128]{3,2,1,0:T(8,128)(2,1)}, bf16[18,8,128,128]{3,2,1,0:T(8,128)(2,1)S(1)}, u32[]{:S(2)}) copy-start(bf16[18,8,128,128]{3,2,1,0:T(8,128)(2,1)S(1)} %copy.46) | copy-start | bytes 14155780
  291.6 13.7 %slice-start = ((s8[4718592]{0:T(1024)(128)(4,1)}), s8[524288]{0:T(1024)(128)(4,1)S(1)}, s32[]{:S(2)}) async-start(s8[4718592]{0:T(1024)(128)(4,1)} %bitcast.78), calls=%async_computation.9 | async-start | bytes 1048576
  291.7 13.7 %slice-start.1 = ((s8[4718592]{0:T(1024)(128)(4,1)}), s8[4194304]{0:T(1024)(128)(4,1)S(1)}, s32[]{:S(2)}) async-start(s8[4718592]{0:T(1024)(128)(4,1)} %bitcast.78), calls=%async_computation.10 | async-start | bytes 8388608
  357.0 122.2 %all-to-all-start.4 = ((bf16[128,2,16384]{2,1,0:T(2,128)(2,1)}), bf16[128,2,16384]{2,1,0:T(2,128)(2,1)}, u32[]{:S(2)}, u32[]{:S(2)}) async-start(bf16[128,2,16384]{2,1,0:T(2,128)(2,1)} %reshape.118), calls=%async_computation.5 | async-start | bytes 16777216 | tf_op jit(solution)/shard_map/all_to_all | solution.py:52
Sparse Core Ops, SparseCore 0:
  61.8 54.9 all-gather.2
  119.1 53.3 all-gather.4
  291.8 134.8 reduce-scatter.1
where the time goes:
time: 516 us; the launch traced here: 509 us
  waiting for transfers between devices  270 us (52%)
  local copies, waits for them, and re-layouts  90 us (17%)
  matrix products  71.4 us (14%)
  starting transfers between devices  50.1 us (10%)
  between operations  15.1 us (3%)
  other arithmetic  12.4 us (2%)
    all_to_all x1, waiting for transfers between devices, collect(): lax.all_to_all(answer_tiles, ('row', 'col'), split_axis=0, concat_axis=0,...  109 us
    all_to_all x1, waiting for transfers between devices, deliver(): lax.all_to_all(sent_tiles, ('row', 'col'), split_axis=0, concat_axis=0, t...  68.2 us
    all_gather x1, waiting for transfers between devices, panel_part(): lax.all_gather(gamma_cols, 'row', axis=1, tiled=True)  55 us
    all_to_all x1, waiting for transfers between devices, panel_part(): lax.all_to_all(gamma_whole, 'col', split_axis=1, concat_axis=0, tiled=True)  36.6 us
    reshape x1, local copies, waits for them, and re-layouts, recoupled_part(): answer.reshape(blocks, capacity, tile_area)  14.2 us
    reshape x1, local copies, waits for them, and re-layouts, recoupled_part(): sent_tiles.reshape(blocks, capacity, tile_area)  14.1 us
    dot_general x1, matrix products, recoupled_part(): jnp.dot(gamma_ph, eta_scaled, preferred_element_type=jnp.float32)  13.7 us
    reshape x1, local copies, waits for them, and re-layouts, recoupled_part(): received = received.reshape(blocks * capacity, tile_area)  13.1 us
  transfers between devices with their start and end apart: 8, of which 4 were waited for; matrix products, arithmetic and copies ran while one was open for 31% of the time, Pallas kernels for 0%

commit v1 on v0

v1 whole, which is shorter than its diff:
```python
import jax
import jax.numpy as jnp
from jax import lax
from jax.experimental import pallas as pl
from jax.experimental.pallas import tpu as pltpu
from jax.sharding import PartitionSpec as P

TILE = 128
ORBITS = 240
PH_STATES = 1536
PH_TILES = 12
PANEL_DEV = 128
ROWS = 1536
COLS = 768
COL_TILES = 6
TILES_BLOCK = 72
SLOTS = 144
BLOCKS = 128
CAP = 2
N_ROW = 8
N_COL = 16
VMEM_LIMIT = 60 * 1024 * 1024

f32 = jnp.float32
bf16 = jnp.bfloat16
SMEM = pltpu.MemorySpace.SMEM
VMEM = pltpu.MemorySpace.VMEM


def smem_spec():
    return pl.BlockSpec(memory_space=SMEM)


def vmem_spec():
    return pl.BlockSpec(memory_space=VMEM)


def params():
    return pltpu.CompilerParams(vmem_limit_bytes=VMEM_LIMIT)


def aligned(start, size):
    return pl.ds(pl.multiple_of(start * size, size), size)


def clear_counts(counts):
    def step(q, carry):
        counts[q] = 0
        return carry

    lax.fori_loop(0, BLOCKS, step, 0)


def buffer_slot(owner_ref, counts, s):
    q = owner_ref[0, s]
    k = counts[q]
    counts[q] = k + 1
    return q * CAP + k


def block_tile(source_ref, s):
    t = source_ref[0, s]
    r = t // COL_TILES
    return aligned(r, TILE), aligned(t - r * COL_TILES, TILE)


def send_kernel(live_ref, source_ref, owner_ref, weight_ref, eta_ref, out_ref, counts):
    clear_counts(counts)

    def step(s, carry):
        n = buffer_slot(owner_ref, counts, s)
        rows, cols = block_tile(source_ref, s)
        out_ref[n] = (weight_ref[0, s] * eta_ref[rows, cols].astype(f32)).astype(bf16)
        return carry

    lax.fori_loop(0, live_ref[0], step, 0)


def update_kernel(live_ref, source_ref, owner_ref, weight_ref, back_ref, out_ref, counts, total):
    clear_counts(counts)

    def first(s, carry):
        n = buffer_slot(owner_ref, counts, s)
        rows, cols = block_tile(source_ref, s)
        total[rows, cols] = weight_ref[0, s] * back_ref[n].astype(f32)
        return carry

    def later(s, carry):
        n = buffer_slot(owner_ref, counts, s)
        rows, cols = block_tile(source_ref, s)
        total[rows, cols] += weight_ref[0, s] * back_ref[n].astype(f32)
        return carry

    lax.fori_loop(0, TILES_BLOCK, first, 0)
    lax.fori_loop(TILES_BLOCK, live_ref[0], later, 0)

    def finish(r, carry):
        rows = aligned(r, TILE)
        out_ref[rows, :] = total[rows, :].astype(bf16)
        return carry

    lax.fori_loop(0, ROWS // TILE, finish, 0)


def channel_kernel(
    code_ref, got_ref, gamma_ref, scale_ref, out_ref, total, eta, eta_scaled, gamma_scaled, product
):
    def clear(r, carry):
        total[aligned(r, TILE), :] = jnp.zeros((TILE, PH_STATES), f32)
        return carry

    lax.fori_loop(0, PH_TILES, clear, 0)

    def place_of(code):
        r = code // PH_TILES
        return aligned(r, TILE), aligned(code - r * PH_TILES, TILE)

    def add(n, carry):
        code = code_ref[n]

        @pl.when(code >= 0)
        def _():
            rows, cols = place_of(code)
            total[rows, cols] += got_ref[n].astype(f32)

        return carry

    lax.fori_loop(0, BLOCKS * CAP, add, 0)

    def scale_rows(r, carry):
        rows = aligned(r, TILE)
        scale = scale_ref[rows, :]
        whole = total[rows, :].astype(bf16)
        eta[rows, :] = whole
        eta_scaled[rows, :] = (-scale * whole.astype(f32)).astype(bf16)
        gamma_scaled[rows, :] = (scale * gamma_ref[rows, :].astype(f32)).astype(bf16)
        return carry

    lax.fori_loop(0, PH_TILES, scale_rows, 0)

    width = 256

    def multiply(c, carry):
        cols = aligned(c, width)
        part = jnp.dot(eta[...], gamma_scaled[:, cols], preferred_element_type=f32)
        part += jnp.dot(gamma_ref[...], eta_scaled[:, cols], preferred_element_type=f32)
        product[:, cols] = part.astype(bf16)
        return carry

    lax.fori_loop(0, PH_STATES // width, multiply, 0)

    def answer(n, carry):
        code = code_ref[n]

        @pl.when(code >= 0)
        def _():
            rows, cols = place_of(code)
            out_ref[n] = product[rows, cols]

        return carry

    lax.fori_loop(0, BLOCKS * CAP, answer, 0)


def panel_kernel(eta_ref, gamma_ref, panel_ref, out_ref):
    gamma_cols = jnp.concatenate([panel_ref[0, 0], panel_ref[1, 0]], axis=1)
    eta_cols = jnp.concatenate([panel_ref[0, 1], panel_ref[1, 1]], axis=1)
    part = jnp.dot(eta_ref[...], gamma_cols, preferred_element_type=f32)
    part -= jnp.dot(gamma_ref[...], eta_cols, preferred_element_type=f32)
    part = part.astype(bf16)
    for k in range(2):
        out_ref[k] = part[:, k * PANEL_DEV : (k + 1) * PANEL_DEV]


def turn_kernel(in_ref, out_ref):
    out_ref[...] = in_ref[...].astype(f32).T.astype(bf16)


def orbit_lookup(pair_ids, occupancy):
    orbit_ids = jnp.arange(occupancy.shape[0], dtype=jnp.int32)
    return jnp.sum(
        jnp.where(pair_ids[:, None] == orbit_ids[None, :], occupancy[None, :], 0.0), axis=1
    )


def panel_part(eta_pairs, gamma_pairs, pair_first, pair_second, occupancy, codes):
    factor = 1.0 - orbit_lookup(pair_first, occupancy) - orbit_lookup(pair_second, occupancy)

    def weigh(pairs):
        return (factor[:, None] * pairs[:, :PANEL_DEV].astype(f32)).astype(bf16)

    halves = jnp.stack([weigh(gamma_pairs), weigh(eta_pairs)]).reshape(2, 2, COLS, PANEL_DEV)
    odd = lax.axis_index("col") % 2 == 1

    def swap(first, second):
        return jnp.where(odd, second, first), jnp.where(odd, first, second)

    def route(flip):
        return [
            (i * N_COL + c, (c // 2) * N_COL + 2 * i + (c + flip) % 2)
            for i in range(N_ROW)
            for c in range(N_COL)
        ]

    same, other = swap(halves[:, 0], halves[:, 1])
    same = lax.ppermute(same, ("row", "col"), route(0))
    other = lax.ppermute(other, ("row", "col"), route(1))
    pieces = jnp.stack(swap(same, other))
    whole = lax.all_gather(
        pieces.reshape(4 * COLS, PANEL_DEV), "row", axis=0, tiled=True
    ).reshape(N_COL, 2, COLS, PANEL_DEV)
    whole, codes = lax.optimization_barrier((whole, codes))
    sums = pl.pallas_call(
        panel_kernel,
        grid=(N_COL // 2,),
        in_specs=[
            pl.BlockSpec((ROWS, COLS), lambda c: (0, 0)),
            pl.BlockSpec((ROWS, COLS), lambda c: (0, 0)),
            pl.BlockSpec((2, 2, COLS, PANEL_DEV), lambda c: (c, 0, 0, 0)),
        ],
        out_specs=pl.BlockSpec((2, ROWS, PANEL_DEV), lambda c: (c, 0, 0)),
        out_shape=jax.ShapeDtypeStruct((N_COL, ROWS, PANEL_DEV), bf16),
        compiler_params=params(),
        cost_estimate=pl.CostEstimate(
            flops=4 * ROWS * COLS * N_COL * PANEL_DEV, bytes_accessed=20 << 20, transcendentals=0
        ),
        name="panel",
    )(eta_pairs, gamma_pairs, whole)
    sums, codes = lax.optimization_barrier((sums, codes))
    done = lax.psum_scatter(
        sums.reshape(N_COL * ROWS, PANEL_DEV), "col", scatter_dimension=0, tiled=True
    )
    return pl.pallas_call(
        turn_kernel,
        in_specs=[vmem_spec()],
        out_specs=vmem_spec(),
        out_shape=jax.ShapeDtypeStruct((PANEL_DEV, ROWS), bf16),
        compiler_params=params(),
        name="turn",
    )(done), codes


def received_codes(owners, places, live):
    slot_ids = jnp.arange(SLOTS, dtype=jnp.int32)
    packed = jnp.where(slot_ids[None, :] < live, owners * 256 + places, -1)
    table = packed
    for axis, size in (("col", N_COL), ("row", N_ROW)):
        place = lax.axis_index(axis)
        span = 1
        while span < size:
            pairs = [(d, d ^ span) for d in range(size)]
            theirs = lax.ppermute(table, axis, pairs)
            upper = (place // span) % 2 == 1
            table = jnp.concatenate(
                [jnp.where(upper, theirs, table), jnp.where(upper, table, theirs)]
            )
            span *= 2
    me = lax.axis_index("row") * N_COL + lax.axis_index("col")
    none = jnp.int32(1 << 20)
    keys = jnp.where((table >> 8) == me, slot_ids[None, :] * 256 + (table & 255), none)
    first = jnp.min(keys, axis=1, keepdims=True)
    second = jnp.min(jnp.where(keys > first, keys, none), axis=1, keepdims=True)
    both = jnp.concatenate([first, second], axis=1)
    return jnp.where(both < none, both & 255, -1).reshape(BLOCKS * CAP)


def exchange(tiles):
    shape = (BLOCKS, CAP * TILE, TILE)
    moved = lax.all_to_all(
        tiles.reshape(shape), ("row", "col"), split_axis=0, concat_axis=0, tiled=True
    )
    return moved.reshape(BLOCKS * CAP, TILE, TILE)


def recoupled_part(
    eta_pairs,
    gamma_recoupled,
    ph_factor,
    tile_source,
    tile_owner,
    tile_place,
    sixj_weight,
    live_count,
    codes,
):
    weights = sixj_weight.astype(f32)
    slots_shape = jax.ShapeDtypeStruct((BLOCKS * CAP, TILE, TILE), bf16)
    counts = pltpu.SMEM((BLOCKS,), jnp.int32)
    sent = pl.pallas_call(
        send_kernel,
        in_specs=[smem_spec()] * 4 + [vmem_spec()],
        out_specs=vmem_spec(),
        out_shape=slots_shape,
        scratch_shapes=[counts],
        compiler_params=params(),
        cost_estimate=pl.CostEstimate(flops=0, bytes_accessed=11 << 20, transcendentals=0),
        name="send",
    )(live_count, tile_source, tile_owner, weights, eta_pairs)
    received = exchange(sent)
    whole = (PH_STATES, PH_STATES)
    answers = pl.pallas_call(
        channel_kernel,
        in_specs=[smem_spec()] + [vmem_spec()] * 3,
        out_specs=vmem_spec(),
        out_shape=slots_shape,
        scratch_shapes=[pltpu.VMEM(whole, f32)] + [pltpu.VMEM(whole, bf16)] * 4,
        compiler_params=params(),
        cost_estimate=pl.CostEstimate(
            flops=4 * PH_STATES**3, bytes_accessed=22 << 20, transcendentals=0
        ),
        name="channel",
    )(codes, received, gamma_recoupled[0], ph_factor.reshape(PH_STATES, 1))
    returned = exchange(answers)
    return pl.pallas_call(
        update_kernel,
        in_specs=[smem_spec()] * 4 + [vmem_spec()],
        out_specs=vmem_spec(),
        out_shape=jax.ShapeDtypeStruct((ROWS, COLS), bf16),
        scratch_shapes=[counts, pltpu.VMEM((ROWS, COLS), f32)],
        compiler_params=params(),
        cost_estimate=pl.CostEstimate(flops=0, bytes_accessed=11 << 20, transcendentals=0),
        name="update",
    )(live_count, tile_source, tile_owner, weights, returned)


def local(
    eta_pairs,
    gamma_pairs,
    pair_first,
    pair_second,
    occupancy,
    gamma_recoupled,
    ph_factor,
    tile_source,
    tile_owner,
    tile_place,
    sixj_weight,
    live_count,
):
    codes = received_codes(tile_owner, tile_place, live_count[0])
    panel_update, codes = panel_part(
        eta_pairs, gamma_pairs, pair_first, pair_second, occupancy, codes
    )
    recoupled_update = recoupled_part(
        eta_pairs,
        gamma_recoupled,
        ph_factor,
        tile_source,
        tile_owner,
        tile_place,
        sixj_weight,
        live_count,
        codes,
    )
    return (panel_update, recoupled_update)


def solution(mesh):
    in_specs = (
        P("row", "col"),
        P("row", "col"),
        P("row"),
        P("row"),
        P(),
        P(("row", "col"), None, None),
        P(("row", "col"), None),
        P(("row", "col"), None),
        P(("row", "col"), None),
        P(("row", "col"), None),
        P(("row", "col"), None),
        P(("row", "col")),
    )
    out_specs = (P("col", "row"), P("row", "col"))
    return jax.shard_map(local, mesh=mesh, in_specs=in_specs, out_specs=out_specs, check_vma=False)
```

time: 516 us -> 381 us (0.74); the launches traced: 509 us -> 381 us
  waiting for transfers between devices: 270 us -> 131 us
  blocking collectives: 0 us -> 112 us
  local copies, waits for them, and re-layouts: 90 us -> 2.72 us
  matrix products: 71.4 us -> 0 us
  Pallas kernels: 0 us -> 70.2 us
  other arithmetic: 12.4 us -> 4.78 us
    all_to_all x5 -> x1, waiting for transfers between devices: 214 us -> 0.01 us  [exchange(): lax.all_to_all(tiles.reshape(shape), ('row', 'col'), split_axis=0, concat...]
    ppermute x0 -> x9, waiting for transfers between devices: none -> 121 us  [the longest x7 89.8 us: received_codes(): theirs = lax.ppermute(table, axis, pairs)]
    all_to_all x0 -> x1, blocking collectives: none -> 112 us  [exchange(): lax.all_to_all(tiles.reshape(shape), ('row', 'col'), split_axis=0, concat...]
    reshape x8 -> x1, local copies, waits for them, and re-layouts: 74.1 us -> 1.18 us  [recoupled_part(): ph_factor.reshape(PH_STATES, 1)]
    dot_general x11 -> x0, matrix products: 71.4 us -> none  [the longest x1 13.7 us: recoupled_part(): jnp.dot(gamma_ph, eta_scaled, preferred_element_type=jnp.float32)]
    pallas_call x0 -> x5, Pallas kernels: none -> 70.2 us  [the longest x1 38.1 us: recoupled_part(): pl.pallas_call(channel_kernel, in_specs=[smem_spec()] + [vmem_spec()] * 3...]
    all_gather x2 -> x1, waiting for transfers between devices: 55 us -> 0.01 us  [panel_part(): lax.all_gather(pieces.reshape(4 * COLS, PANEL_DEV), 'row', axis=0, tiled=...]
    all_to_all x5 -> x1, starting transfers between devices: 49.8 us -> 13.4 us  [exchange(): lax.all_to_all(tiles.reshape(shape), ('row', 'col'), split_axis=0, concat...]
  transfers between devices with their start and end apart: 8 -> 12, of which waited for: 4 -> 10; matrix products, arithmetic and copies ran while one was open for 31% -> 1% of each run, Pallas kernels for 0% -> 16%
where the time goes in v1:
time: 381 us
  waiting for transfers between devices  131 us (34%)
  blocking collectives  112 us (29%)
  Pallas kernels  70.2 us (18%)
  starting transfers between devices  46.3 us (12%)
  between operations  14.9 us (4%)
  other arithmetic  4.78 us (1%)
    all_to_all x1, blocking collectives, exchange(): lax.all_to_all(tiles.reshape(shape), ('row', 'col'), split_axis=0, concat...  112 us
    ppermute x7, waiting for transfers between devices, received_codes(): theirs = lax.ppermute(table, axis, pairs)  89.8 us
    pallas_call x1, Pallas kernels, recoupled_part(): pl.pallas_call(channel_kernel, in_specs=[smem_spec()] + [vmem_spec()] * 3...  38.1 us
    ppermute x7, starting transfers between devices, received_codes(): theirs = lax.ppermute(table, axis, pairs)  26.5 us
    ppermute x1, waiting for transfers between devices, panel_part(): same = lax.ppermute(same, ('row', 'col'), route(0))  19.3 us
    pallas_call x1, Pallas kernels, panel_part(): pl.pallas_call(panel_kernel, grid=(N_COL // 2,), in_specs=[pl.BlockSpec((...  14.8 us
    all_to_all x1, starting transfers between devices, exchange(): lax.all_to_all(tiles.reshape(shape), ('row', 'col'), split_axis=0, concat...  13.4 us
    ppermute x1, waiting for transfers between devices, panel_part(): other = lax.ppermute(other, ('row', 'col'), route(1))  12.4 us
  transfers between devices with their start and end apart: 12, of which 10 were waited for; matrix products, arithmetic and copies ran while one was open for 1% of the time, Pallas kernels for 16%

profile of v1, /device:TPU:8, one launch (start us, length us, event | category | flops | bytes accessed | tf_op | source)
XLA Modules:
  0.0 381.4 jit_solution(4590085604531321806)
XLA Ops:
  7.2 0.0 all-gather.2.cloned.1.call-start
  7.2 1.2 select_reduce_fusion.1
  8.5 1.4 multiply_convert_fusion.1
  9.9 0.1 fusion.2
  10.0 0.0 copy-start.3
  10.0 2.8 collective-permute-start
  12.8 0.1 fusion
  12.9 3.5 collective-permute-start.1
  16.3 12.4 %collective-permute-done = bf16[2,768,128]{2,1,0:T(8,128)(2,1)S(1)} collective-permute-done((bf16[2,768,128]{2,1,0:T(8,128)(2,1)S(1)}, bf16[2,768,128]{2,1,0:T(8,128)(2,1)S(1)}, u32[]{:S(2)}, u32[]{:S(2)}) %collective-permute-start) | collective-permute-done | bytes 393248 | tf_op jit(solution)/shard_map/ppermute | solution.py:207
  28.7 19.3 %collective-permute-done.1 = bf16[2,768,128]{2,1,0:T(8,128)(2,1)S(1)} collective-permute-done((bf16[2,768,128]{2,1,0:T(8,128)(2,1)S(1)}, bf16[2,768,128]{2,1,0:T(8,128)(2,1)S(1)}, u32[]{:S(2)}, u32[]{:S(2)}) %collective-permute-start.1) | collective-permute-done | bytes 393248 | tf_op jit(solution)/shard_map/ppermute | solution.py:206
  48.0 0.1 select_bitcast_fusion.1
  48.0 0.9 pad_maximum_fusion
  49.0 0.0 all-gather.2.cloned.1.call-update
  49.6 0.0 copy-done.3
  49.7 0.6 convert_element_type.19.weight_ref
  50.2 7.6 %send.1 = bf16[256,128,128]{2,1,0:T(8,128)(2,1)} custom-call(s32[1]{0:T(128)} %copy.31.live_ref, s32[1,144]{1,0:T(1,128)} %source_ref.3, s32[1,144]{1,0:T(1,128)} %owner_ref.3, f32[1,144]{1,0:T(1,128)} %convert_element_type.19.weight_ref, bf16[1536,768]{1,0:T(8,128)(2,1)} %eta_ref.3), custom_call_target="tpu_custom_call" | custom-call | bytes 11534336 | tf_op jit(solution)/shard_map/send/pallas_call | solution.py:289
  57.8 0.0 copy-start
  57.8 0.0 copy-start.2
  57.8 13.4 %all-to-all-start = ((bf16[128,256,128]{2,1,0:T(8,128)(2,1)}), bf16[128,256,128]{2,1,0:T(8,128)(2,1)}, u32[]{:S(2)}, u32[]{:S(2)}) async-start(bf16[128,256,128]{2,1,0:T(8,128)(2,1)} %bitcast.35), calls=%async_computation.1 | async-start | bytes 16777216 | tf_op jit(solution)/shard_map/all_to_all | solution.py:269
  71.2 0.0 reduce-scatter.2.cloned.1.call-start
  71.3 0.0 copy-done
  71.3 0.0 copy-done.2
  71.3 1.7 collective-permute-start.2
  73.0 38.2 %collective-permute-done.2 = s32[1,144]{1,0:T(1,128)S(1)} collective-permute-done((s32[1,144]{1,0:T(1,128)S(1)}, s32[1,144]{1,0:T(1,128)S(1)}, u32[]{:S(2)}, u32[]{:S(2)}) %collective-permute-start.2) | collective-permute-done | bytes 608 | tf_op jit(solution)/shard_map/ppermute | solution.py:252
  111.2 0.7 collective-permute-start.3
  112.0 4.4 %collective-permute-done.3 = s32[2,144]{1,0:T(2,128)S(1)} collective-permute-done((s32[2,144]{1,0:T(2,128)S(1)}, s32[2,144]{1,0:T(2,128)S(1)}, u32[]{:S(2)}, u32[]{:S(2)}) %collective-permute-start.3) | collective-permute-done | bytes 1184 | tf_op jit(solution)/shard_map/ppermute | solution.py:252
  116.4 11.0 %collective-permute-start.4 = (s32[4,144]{1,0:T(4,128)S(1)}, s32[4,144]{1,0:T(4,128)S(1)}, u32[]{:S(2)}, u32[]{:S(2)}) collective-permute-start(s32[4,144]{1,0:T(4,128)S(1)} %pad_add_fusion.5), channel_id=1, source_target_pairs={{0,4},{1,5},{2,6},{3,7},{4,0},{5,1},{6,2},{7,3},{8,12},{9,13},{10,... | collective-permute-start | bytes 6920 | tf_op jit(solution)/shard_map/ppermute | solution.py:252
  127.5 1.6 collective-permute-done.4
  129.1 8.4 %collective-permute-start.5 = (s32[8,144]{1,0:T(8,128)S(1)}, s32[8,144]{1,0:T(8,128)S(1)}, u32[]{:S(2)}, u32[]{:S(2)}) collective-permute-start(s32[8,144]{1,0:T(8,128)S(1)} %pad_add_fusion.4), channel_id=1, source_target_pairs={{0,8},{1,9},{2,10},{3,11},{4,12},{5,13},{6,14},{7,15},{8,0},{9,1},... | collective-permute-start | bytes 13832 | tf_op jit(solution)/shard_map/ppermute | solution.py:252
  137.5 1.7 collective-permute-done.5
  139.3 0.1 collective-permute-start.6
  139.4 1.2 collective-permute-done.6
  140.6 2.4 collective-permute-start.7
  143.0 38.8 %collective-permute-done.7 = s32[32,144]{1,0:T(8,128)S(1)} collective-permute-done((s32[32,144]{1,0:T(8,128)S(1)}, s32[32,144]{1,0:T(8,128)S(1)}, u32[]{:S(2)}, u32[]{:S(2)}) %collective-permute-start.7) | collective-permute-done | bytes 18464 | tf_op jit(solution)/shard_map/ppermute | solution.py:252
  181.9 2.1 collective-permute-start.8
  184.0 3.8 collective-permute-done.8
  187.8 0.1 fusion.4
  187.9 0.2 fusion.3
  188.1 0.1 copy.28
  188.2 0.7 select_n.236.code_ref
  188.9 0.0 all-gather.2.cloned.1.call-done
  188.9 14.8 %panel.1 = bf16[16,1536,128]{2,1,0:T(8,128)(2,1)} custom-call(bf16[1536,768]{1,0:T(8,128)(2,1)} %eta_ref.3, bf16[1536,768]{1,0:T(8,128)(2,1)} %gamma_ref.1, bf16[16,2,768,128]{3,2,1,0:T(8,128)(2,1)} %bitcast.47), custom_call_target="tpu_custom_call" | custom-call | flops 9663676416 | bytes 20971520 | tf_op jit(solution)/shard_map/panel/pallas_call | solution.py:213
  203.8 0.0 copy-start.1
  203.8 0.0 reduce-scatter.2.cloned.1.call-update
  203.8 0.7 copy-done.1
  204.5 1.2 copy.29.scale_ref
  205.7 0.0 all-to-all-done
  205.7 38.1 %channel.1 = bf16[256,128,128]{2,1,0:T(8,128)(2,1)} custom-call(s32[256]{0:T(256)} %select_n.236.code_ref, bf16[256,128,128]{2,1,0:T(8,128)(2,1)} %bitcast.16.got_ref, bf16[1536,1536]{1,0:T(8,128)(2,1)} %bitcast.48, f32[1536,1]{1,0:T(8,128)} %copy.29.scale_ref), custom_call_target="tpu_custom_call" | custom-call | flops 14495514624 | bytes 23068672 | tf_op jit(solution)/shard_map/channel/pallas_call | solution.py:301
  243.7 111.9 %all_to_all.10 = bf16[128,256,128]{2,1,0:T(8,128)(2,1)} all-to-all(bf16[128,256,128]{2,1,0:T(8,128)(2,1)} %bitcast.37), channel_id=1, replica_groups=mesh['row'=8,'col'=16] {'row','col'}, dimensions={0} | all-to-all | bytes 16777216 | tf_op jit(solution)/shard_map/all_to_all | solution.py:269
  355.7 7.8 %update.1 = bf16[1536,768]{1,0:T(8,128)(2,1)} custom-call(s32[1]{0:T(128)} %copy.31.live_ref, s32[1,144]{1,0:T(1,128)} %source_ref.3, s32[1,144]{1,0:T(1,128)} %owner_ref.3, f32[1,144]{1,0:T(1,128)} %convert_element_type.19.weight_ref, bf16[256,128,128]{2,1,0:T(8,128)(2,1)} %bitcast.36), custom_call_target="tpu_custom_call" | custom-call | bytes 11534336 | tf_op jit(solution)/shard_map/update/pallas_call | solution.py:314
  363.4 9.3 %reduce-scatter.2.cloned.1.call-done.in_ref = bf16[1536,128]{1,0:T(8,128)(2,1)} async-done(((bf16[24576,128]{1,0:T(8,128)(2,1)}), bf16[1536,128]{1,0:T(8,128)(2,1)}) %reduce-scatter.2.cloned.1.call-update) | async-done | bytes 393232 | tf_op jit(solution)/shard_map/reduce_scatter | solution.py:230
  372.7 1.9 turn.1
  (17 shorter events, 0.1 us)
Async XLA Ops:
  7.2 181.8 %all-gather.2.cloned.1.call-start = ((), (), s32[]{:S(2)}) async-start(), calls=%async_computation.3 | async-start | bytes 7077888 | tf_op jit(solution)/shard_map/all_gather | solution.py:209
  10.0 39.7 %copy-start.3 = (bf16[1,144]{1,0:T(2,128)(2,1)S(1)}, bf16[1,144]{1,0:T(2,128)(2,1)}, u32[]{:S(2)}) copy-start(bf16[1,144]{1,0:T(2,128)(2,1)} %param.22) | copy-start | bytes 868
  10.0 18.7 %collective-permute-start = (bf16[2,768,128]{2,1,0:T(8,128)(2,1)S(1)}, bf16[2,768,128]{2,1,0:T(8,128)(2,1)S(1)}, u32[]{:S(2)}, u32[]{:S(2)}) collective-permute-start(bf16[2,768,128]{2,1,0:T(8,128)(2,1)S(1)} %fusion.2), channel_id=1, source_target_pairs={{0,1},{1,0},{2,17},{3,16},{4,33},{5,32},{6,49},{7,48},{8,65},{9,64... | collective-permute-start | bytes 1179656 | tf_op jit(solution)/shard_map/ppermute | solution.py:207
  12.9 35.1 %collective-permute-start.1 = (bf16[2,768,128]{2,1,0:T(8,128)(2,1)S(1)}, bf16[2,768,128]{2,1,0:T(8,128)(2,1)S(1)}, u32[]{:S(2)}, u32[]{:S(2)}) collective-permute-start(bf16[2,768,128]{2,1,0:T(8,128)(2,1)S(1)} %fusion), channel_id=1, source_target_pairs={{0,0},{1,1},{2,16},{3,17},{4,32},{5,33},{6,48},{7,49},{8,64},{9,65... | collective-permute-start | bytes 1179656 | tf_op jit(solution)/shard_map/ppermute | solution.py:206
  57.8 13.5 %copy-start = (s32[1,144]{1,0:T(1,128)S(1)}, s32[1,144]{1,0:T(1,128)}, u32[]{:S(2)}) copy-start(s32[1,144]{1,0:T(1,128)} %owner_ref.3) | copy-start | bytes 1732
  57.8 13.5 %copy-start.2 = (s32[1,144]{1,0:T(1,128)S(1)}, s32[1,144]{1,0:T(1,128)}, u32[]{:S(2)}) copy-start(s32[1,144]{1,0:T(1,128)} %param.21) | copy-start | bytes 1732
  57.8 147.8 %all-to-all-start = ((bf16[128,256,128]{2,1,0:T(8,128)(2,1)}), bf16[128,256,128]{2,1,0:T(8,128)(2,1)}, u32[]{:S(2)}, u32[]{:S(2)}) async-start(bf16[128,256,128]{2,1,0:T(8,128)(2,1)} %bitcast.35), calls=%async_computation.1 | async-start | bytes 16777216 | tf_op jit(solution)/shard_map/all_to_all | solution.py:269
  71.2 301.5 %reduce-scatter.2.cloned.1.call-start = ((), (), s32[]{:S(2)}) async-start(), calls=%async_computation.4 | async-start | bytes 6684672 | tf_op jit(solution)/shard_map/reduce_scatter | solution.py:230
  71.3 39.9 %collective-permute-start.2 = (s32[1,144]{1,0:T(1,128)S(1)}, s32[1,144]{1,0:T(1,128)S(1)}, u32[]{:S(2)}, u32[]{:S(2)}) collective-permute-start(s32[1,144]{1,0:T(1,128)S(1)} %compare_select_fusion.1), channel_id=1, source_target_pairs={{0,1},{1,0},{2,3},{3,2},{4,5},{5,4},{6,7},{7,6},{8,9},{9,8},{10,11... | collective-permute-start | bytes 1736 | tf_op jit(solution)/shard_map/ppermute | solution.py:252
  111.2 5.2 %collective-permute-start.3 = (s32[2,144]{1,0:T(2,128)S(1)}, s32[2,144]{1,0:T(2,128)S(1)}, u32[]{:S(2)}, u32[]{:S(2)}) collective-permute-start(s32[2,144]{1,0:T(2,128)S(1)} %pad_add_fusion.6), channel_id=1, source_target_pairs={{0,2},{1,3},{2,0},{3,1},{4,6},{5,7},{6,4},{7,5},{8,10},{9,11},{10,... | collective-permute-start | bytes 3464 | tf_op jit(solution)/shard_map/ppermute | solution.py:252
  116.4 12.6 %collective-permute-start.4 = (s32[4,144]{1,0:T(4,128)S(1)}, s32[4,144]{1,0:T(4,128)S(1)}, u32[]{:S(2)}, u32[]{:S(2)}) collective-permute-start(s32[4,144]{1,0:T(4,128)S(1)} %pad_add_fusion.5), channel_id=1, source_target_pairs={{0,4},{1,5},{2,6},{3,7},{4,0},{5,1},{6,2},{7,3},{8,12},{9,13},{10,... | collective-permute-start | bytes 6920 | tf_op jit(solution)/shard_map/ppermute | solution.py:252
  129.1 10.2 %collective-permute-start.5 = (s32[8,144]{1,0:T(8,128)S(1)}, s32[8,144]{1,0:T(8,128)S(1)}, u32[]{:S(2)}, u32[]{:S(2)}) collective-permute-start(s32[8,144]{1,0:T(8,128)S(1)} %pad_add_fusion.4), channel_id=1, source_target_pairs={{0,8},{1,9},{2,10},{3,11},{4,12},{5,13},{6,14},{7,15},{8,0},{9,1},... | collective-permute-start | bytes 13832 | tf_op jit(solution)/shard_map/ppermute | solution.py:252
  139.3 1.3 collective-permute-start.6
  140.6 41.3 %collective-permute-start.7 = (s32[32,144]{1,0:T(8,128)S(1)}, s32[32,144]{1,0:T(8,128)S(1)}, u32[]{:S(2)}, u32[]{:S(2)}) collective-permute-start(s32[32,144]{1,0:T(8,128)S(1)} %pad_add_fusion.2), channel_id=1, source_target_pairs={{0,32},{16,48},{32,0},{48,16},{64,96},{80,112},{96,64},{112,80},{1... | collective-permute-start | bytes 55304 | tf_op jit(solution)/shard_map/ppermute | solution.py:252
  181.9 5.8 %collective-permute-start.8 = (s32[64,144]{1,0:T(8,128)S(1)}, s32[64,144]{1,0:T(8,128)S(1)}, u32[]{:S(2)}, u32[]{:S(2)}) collective-permute-start(s32[64,144]{1,0:T(8,128)S(1)} %pad_add_fusion.1), channel_id=1, source_target_pairs={{0,64},{16,80},{32,96},{48,112},{64,0},{80,16},{96,32},{112,48},{1... | collective-permute-start | bytes 110600 | tf_op jit(solution)/shard_map/ppermute | solution.py:252
  203.8 0.7 copy-start.1
Sparse Core Ops, SparseCore 0:
  49.1 76.2 all-gather.1
  203.9 168.7 reduce-scatter.1

commit v2 on v1

v2 whole, which is shorter than its diff:
```python
import jax
import jax.numpy as jnp
from jax import lax
from jax.experimental import pallas as pl
from jax.experimental.pallas import tpu as pltpu
from jax.sharding import PartitionSpec as P

TILE = 128
ORBITS = 240
PH_STATES = 1536
PH_TILES = 12
PANEL_DEV = 128
ROWS = 1536
COLS = 768
COL_TILES = 6
TILES_BLOCK = 72
SLOTS = 144
BLOCKS = 128
CAP = 2
N_ROW = 8
N_COL = 16
GROUP = 16
CODE_ROWS = 8
VMEM_LIMIT = 60 * 1024 * 1024

f32 = jnp.float32
bf16 = jnp.bfloat16
SMEM = pltpu.MemorySpace.SMEM
VMEM = pltpu.MemorySpace.VMEM


def smem_spec():
    return pl.BlockSpec(memory_space=SMEM)


def any_spec():
    return pl.BlockSpec(memory_space=pl.ANY)


def vmem_spec():
    return pl.BlockSpec(memory_space=VMEM)


def params():
    return pltpu.CompilerParams(vmem_limit_bytes=VMEM_LIMIT)


def aligned(start, size):
    return pl.ds(pl.multiple_of(start * size, size), size)


def step_through(count, unroll, body):
    def step(i, carry):
        for j in range(unroll):
            body(i * unroll + j)
        return carry

    lax.fori_loop(0, count // unroll, step, 0)


def send_kernel(
    live_ref,
    source_ref,
    owner_ref,
    place_ref,
    weight_ref,
    eta_ref,
    out_ref,
    tile_ref,
    factor_ref,
    place_of,
    counts,
    held,
    sems,
):
    def clear(n):
        tile_ref[n] = 0
        factor_ref[n] = 0.0
        place_of[n] = 0

    step_through(BLOCKS * CAP, 8, clear)

    def clear_count(q):
        counts[q] = 0

    step_through(BLOCKS, 8, clear_count)

    def slot(s, carry):
        q = owner_ref[0, s]
        k = counts[q]
        counts[q] = k + 1
        n = q * CAP + k
        t = source_ref[0, s]
        r = t // COL_TILES
        tile_ref[n] = r * 8 + (t - r * COL_TILES)
        factor_ref[n] = weight_ref[0, s]
        place_of[n] = place_ref[0, s]
        return carry

    lax.fori_loop(0, live_ref[0], slot, 0)
    lane = lax.broadcasted_iota(jnp.int32, (CODE_ROWS, TILE), 1)

    def copy(j):
        part = pl.ds(j * GROUP, GROUP)
        return pltpu.make_async_copy(held.at[part], out_ref.at[part], sems.at[j])

    def group(j, carry):
        def owner(i):
            q = j * GROUP + i
            for k in range(CAP):
                n = q * CAP + k
                t = tile_ref[n]
                tile = eta_ref[aligned(t >> 3, TILE), aligned(t & 7, TILE)]
                held[q, k * TILE : (k + 1) * TILE, :] = (
                    factor_ref[n] * tile.astype(f32)
                ).astype(bf16)
            codes = jnp.where(lane == 0, place_of[q * CAP], place_of[q * CAP + 1])
            held[q, CAP * TILE : CAP * TILE + CODE_ROWS, :] = codes.astype(f32).astype(bf16)

        step_through(GROUP, 4, owner)
        copy(j).start()
        return carry

    lax.fori_loop(0, BLOCKS // GROUP, group, 0)

    def finish(j):
        copy(j).wait()

    step_through(BLOCKS // GROUP, 1, finish)


def update_kernel(tile_ref, factor_ref, back_ref, out_ref, held, total, sems):
    def copy(j):
        part = pl.ds(j * GROUP, GROUP)
        return pltpu.make_async_copy(back_ref.at[part], held.at[part], sems.at[j])

    def begin(j):
        copy(j).start()

    step_through(BLOCKS // GROUP, 1, begin)

    def clear(r):
        total[aligned(r, TILE), :] = jnp.zeros((TILE, COLS), f32)

    step_through(ROWS // TILE, 1, clear)

    def group(j, carry):
        copy(j).wait()

        def owner(i):
            q = j * GROUP + i
            for k in range(CAP):
                n = q * CAP + k
                t = tile_ref[n]
                rows, cols = aligned(t >> 3, TILE), aligned(t & 7, TILE)
                total[rows, cols] += factor_ref[n] * held[
                    q, k * TILE : (k + 1) * TILE, :
                ].astype(f32)

        step_through(GROUP, 4, owner)
        return carry

    lax.fori_loop(0, BLOCKS // GROUP, group, 0)

    def finish(r):
        rows = aligned(r, TILE)
        out_ref[rows, :] = total[rows, :].astype(bf16)

    step_through(ROWS // TILE, 1, finish)


def channel_kernel(
    place_ref,
    got_ref,
    gamma_hbm,
    scale_ref,
    out_ref,
    held,
    gamma_ref,
    total,
    eta,
    product,
    got_sems,
    gamma_sem,
    out_sems,
):
    def copy(j):
        part = pl.ds(j * GROUP, GROUP)
        return pltpu.make_async_copy(
            got_ref.at[part, pl.ds(0, CAP * TILE)], held.at[part], got_sems.at[j]
        )

    gamma_copy = pltpu.make_async_copy(gamma_hbm, gamma_ref, gamma_sem)

    def begin(j):
        copy(j).start()

    step_through(BLOCKS // GROUP, 1, begin)
    gamma_copy.start()

    def clear(r):
        total[aligned(r, TILE), :] = jnp.zeros((TILE, PH_STATES), f32)

    step_through(PH_TILES, 1, clear)

    def place(n):
        code = place_ref[n]
        return aligned(code >> 4, TILE), aligned(code & 15, TILE)

    def group(j, carry):
        copy(j).wait()

        def block(i):
            b = j * GROUP + i
            for k in range(CAP):
                rows, cols = place(b * CAP + k)
                total[rows, cols] += held[b, k * TILE : (k + 1) * TILE, :].astype(f32)

        step_through(GROUP, 4, block)
        return carry

    lax.fori_loop(0, BLOCKS // GROUP, group, 0)

    def settle(r):
        rows = aligned(r, TILE)
        eta[rows, :] = total[rows, :].astype(bf16)

    step_through(PH_TILES, 1, settle)
    gamma_copy.wait()
    width = 256

    def multiply(c):
        cols = aligned(c, width)
        scale = scale_ref[...]
        gamma_scaled = (scale * gamma_ref[:, cols].astype(f32)).astype(bf16)
        eta_scaled = (-scale * eta[:, cols].astype(f32)).astype(bf16)
        part = jnp.dot(eta[...], gamma_scaled, preferred_element_type=f32)
        part += jnp.dot(gamma_ref[...], eta_scaled, preferred_element_type=f32)
        product[:, cols] = part.astype(bf16)

    step_through(PH_STATES // width, 1, multiply)

    def back(j):
        part = pl.ds(j * GROUP, GROUP)
        return pltpu.make_async_copy(held.at[part], out_ref.at[part], out_sems.at[j])

    def answers(j, carry):
        def block(i):
            b = j * GROUP + i
            for k in range(CAP):
                rows, cols = place(b * CAP + k)
                held[b, k * TILE : (k + 1) * TILE, :] = product[rows, cols]

        step_through(GROUP, 4, block)
        back(j).start()
        return carry

    lax.fori_loop(0, BLOCKS // GROUP, answers, 0)

    def finish(j):
        back(j).wait()

    step_through(BLOCKS // GROUP, 1, finish)


def panel_kernel(eta_ref, gamma_ref, panel_ref, out_ref):
    gamma_cols = jnp.concatenate([panel_ref[0, 0], panel_ref[1, 0]], axis=1)
    eta_cols = jnp.concatenate([panel_ref[0, 1], panel_ref[1, 1]], axis=1)
    part = jnp.dot(eta_ref[...], gamma_cols, preferred_element_type=f32)
    part -= jnp.dot(gamma_ref[...], eta_cols, preferred_element_type=f32)
    part = part.astype(bf16)
    for k in range(2):
        out_ref[k] = part[:, k * PANEL_DEV : (k + 1) * PANEL_DEV]


def turn_kernel(in_ref, out_ref):
    out_ref[...] = in_ref[...].astype(f32).T.astype(bf16)


def orbit_lookup(pair_ids, occupancy):
    orbit_ids = jnp.arange(occupancy.shape[0], dtype=jnp.int32)
    return jnp.sum(
        jnp.where(pair_ids[:, None] == orbit_ids[None, :], occupancy[None, :], 0.0), axis=1
    )


def panel_pieces(eta_pairs, gamma_pairs, pair_first, pair_second, occupancy):
    factor = 1.0 - orbit_lookup(pair_first, occupancy) - orbit_lookup(pair_second, occupancy)

    def weigh(pairs):
        return (factor[:, None] * pairs[:, :PANEL_DEV].astype(f32)).astype(bf16)

    halves = jnp.stack([weigh(gamma_pairs), weigh(eta_pairs)]).reshape(2, 2, COLS, PANEL_DEV)
    odd = lax.axis_index("col") % 2 == 1

    def swap(first, second):
        return jnp.where(odd, second, first), jnp.where(odd, first, second)

    def route(flip):
        return [
            (i * N_COL + c, (c // 2) * N_COL + 2 * i + (c + flip) % 2)
            for i in range(N_ROW)
            for c in range(N_COL)
        ]

    same, other = swap(halves[:, 0], halves[:, 1])
    same = lax.ppermute(same, ("row", "col"), route(0))
    other = lax.ppermute(other, ("row", "col"), route(1))
    return jnp.stack(swap(same, other))


def panel_part(eta_pairs, gamma_pairs, pieces):
    whole = lax.all_gather(
        pieces.reshape(4 * COLS, PANEL_DEV), "row", axis=0, tiled=True
    ).reshape(N_COL, 2, COLS, PANEL_DEV)
    sums = pl.pallas_call(
        panel_kernel,
        grid=(N_COL // 2,),
        in_specs=[
            pl.BlockSpec((ROWS, COLS), lambda c: (0, 0)),
            pl.BlockSpec((ROWS, COLS), lambda c: (0, 0)),
            pl.BlockSpec((2, 2, COLS, PANEL_DEV), lambda c: (c, 0, 0, 0)),
        ],
        out_specs=pl.BlockSpec((2, ROWS, PANEL_DEV), lambda c: (c, 0, 0)),
        out_shape=jax.ShapeDtypeStruct((N_COL, ROWS, PANEL_DEV), bf16),
        compiler_params=params(),
        cost_estimate=pl.CostEstimate(
            flops=4 * ROWS * COLS * N_COL * PANEL_DEV, bytes_accessed=20 << 20, transcendentals=0
        ),
        name="panel",
    )(eta_pairs, gamma_pairs, whole)
    done = lax.psum_scatter(
        sums.reshape(N_COL * ROWS, PANEL_DEV), "col", scatter_dimension=0, tiled=True
    )
    return pl.pallas_call(
        turn_kernel,
        in_specs=[vmem_spec()],
        out_specs=vmem_spec(),
        out_shape=jax.ShapeDtypeStruct((PANEL_DEV, ROWS), bf16),
        compiler_params=params(),
        name="turn",
    )(done)


def exchange(tiles):
    return lax.all_to_all(tiles, ("row", "col"), split_axis=0, concat_axis=0, tiled=True)


def updates(
    eta_pairs,
    gamma_pairs,
    pieces,
    gamma_recoupled,
    ph_factor,
    tile_source,
    tile_owner,
    tile_place,
    sixj_weight,
    live_count,
):
    weights = sixj_weight.astype(f32)
    slots = BLOCKS * CAP
    groups = BLOCKS // GROUP
    rows = CAP * TILE
    dma = pltpu.SemaphoreType.DMA
    held = pltpu.VMEM((BLOCKS, rows, TILE), bf16)
    sent, tiles, factors = pl.pallas_call(
        send_kernel,
        in_specs=[smem_spec()] * 5 + [vmem_spec()],
        out_specs=[any_spec(), smem_spec(), smem_spec()],
        out_shape=[
            jax.ShapeDtypeStruct((BLOCKS, rows + CODE_ROWS, TILE), bf16),
            jax.ShapeDtypeStruct((slots,), jnp.int32),
            jax.ShapeDtypeStruct((slots,), f32),
        ],
        scratch_shapes=[
            pltpu.SMEM((slots,), jnp.int32),
            pltpu.SMEM((BLOCKS,), jnp.int32),
            pltpu.VMEM((BLOCKS, rows + CODE_ROWS, TILE), bf16),
            dma((groups,)),
        ],
        compiler_params=params(),
        cost_estimate=pl.CostEstimate(flops=0, bytes_accessed=11 << 20, transcendentals=0),
        name="send",
    )(live_count, tile_source, tile_owner, tile_place, weights, eta_pairs)
    sent, pieces = lax.optimization_barrier((sent, pieces))
    panel_update = panel_part(eta_pairs, gamma_pairs, pieces)
    received = exchange(sent)
    places = received[:, rows, :CAP].astype(jnp.int32).reshape(slots)
    places = places // PH_TILES * 16 + places % PH_TILES
    whole = (PH_STATES, PH_STATES)
    answers = pl.pallas_call(
        channel_kernel,
        in_specs=[smem_spec(), any_spec(), any_spec(), vmem_spec()],
        out_specs=any_spec(),
        out_shape=jax.ShapeDtypeStruct((BLOCKS, rows, TILE), bf16),
        scratch_shapes=[
            held,
            pltpu.VMEM(whole, bf16),
            pltpu.VMEM(whole, f32),
            pltpu.VMEM(whole, bf16),
            pltpu.VMEM(whole, bf16),
            dma((groups,)),
            dma,
            dma((groups,)),
        ],
        compiler_params=params(),
        cost_estimate=pl.CostEstimate(
            flops=4 * PH_STATES**3, bytes_accessed=22 << 20, transcendentals=0
        ),
        name="channel",
    )(places, received, gamma_recoupled[0], ph_factor.reshape(PH_STATES, 1))
    returned = exchange(answers)
    recoupled_update = pl.pallas_call(
        update_kernel,
        in_specs=[smem_spec(), smem_spec(), any_spec()],
        out_specs=vmem_spec(),
        out_shape=jax.ShapeDtypeStruct((ROWS, COLS), bf16),
        scratch_shapes=[held, pltpu.VMEM((ROWS, COLS), f32), dma((groups,))],
        compiler_params=params(),
        cost_estimate=pl.CostEstimate(flops=0, bytes_accessed=11 << 20, transcendentals=0),
        name="update",
    )(tiles, factors, returned)
    return (panel_update, recoupled_update)


def local(
    eta_pairs,
    gamma_pairs,
    pair_first,
    pair_second,
    occupancy,
    gamma_recoupled,
    ph_factor,
    tile_source,
    tile_owner,
    tile_place,
    sixj_weight,
    live_count,
):
    pieces = panel_pieces(eta_pairs, gamma_pairs, pair_first, pair_second, occupancy)
    return updates(
        eta_pairs,
        gamma_pairs,
        pieces,
        gamma_recoupled,
        ph_factor,
        tile_source,
        tile_owner,
        tile_place,
        sixj_weight,
        live_count,
    )


def solution(mesh):
    in_specs = (
        P("row", "col"),
        P("row", "col"),
        P("row"),
        P("row"),
        P(),
        P(("row", "col"), None, None),
        P(("row", "col"), None),
        P(("row", "col"), None),
        P(("row", "col"), None),
        P(("row", "col"), None),
        P(("row", "col"), None),
        P(("row", "col")),
    )
    out_specs = (P("col", "row"), P("row", "col"))
    return jax.shard_map(local, mesh=mesh, in_specs=in_specs, out_specs=out_specs, check_vma=False)
```

time: 381 us -> 347 us (0.911)
  starting transfers between devices: 46.3 us -> 17.6 us
  Pallas kernels: 70.2 us -> 58.3 us
    ppermute x9 -> x2, waiting for transfers between devices: 121 us -> 21.7 us  [the longest x1 19.3 us: panel_pieces(): same = lax.ppermute(same, ('row', 'col'), route(0))]
    all_gather x1, waiting for transfers between devices: 0.01 us -> 85.8 us  [panel_part(): lax.all_gather(pieces.reshape(4 * COLS, PANEL_DEV), 'row', axis=0, tiled=...]
    ppermute x9 -> x2, starting transfers between devices: 32.8 us -> 6.27 us  [the longest x1 3.46 us: panel_pieces(): same = lax.ppermute(same, ('row', 'col'), route(0))]
    all_to_all x1, waiting for transfers between devices: 0.01 us -> 23 us  [exchange(): lax.all_to_all(tiles, ('row', 'col'), split_axis=0, concat_axis=0, tiled=...]
    pallas_call x3, Pallas kernels: 53.4 us -> 41.5 us  [the longest x1 26.7 us: updates(): pl.pallas_call(channel_kernel, in_specs=[smem_spec(), any_spec(), any_spe...]
    reduce_scatter x1, waiting for transfers between devices: 9.25 us -> 0.02 us  [panel_part(): lax.psum_scatter(sums.reshape(N_COL * ROWS, PANEL_DEV), 'col', scatter_di...]
  transfers between devices with their start and end apart: 12 -> 5, of which waited for: 10 -> 4; matrix products, arithmetic and copies ran while one was open for 1% -> 2% of each run, Pallas kernels for 16% -> 14%
where the time goes in v2:
time: 347 us; the launch traced here: 344 us
  waiting for transfers between devices  131 us (38%)
  blocking collectives  113 us (33%)
  Pallas kernels  58.3 us (17%)
  starting transfers between devices  17.6 us (5%)
  between operations  14.8 us (4%)
  other arithmetic  7.74 us (2%)
    all_to_all x1, blocking collectives, exchange(): lax.all_to_all(tiles, ('row', 'col'), split_axis=0, concat_axis=0, tiled=...  113 us
    all_gather x1, waiting for transfers between devices, panel_part(): lax.all_gather(pieces.reshape(4 * COLS, PANEL_DEV), 'row', axis=0, tiled=...  85.8 us
    pallas_call x1, Pallas kernels, updates(): pl.pallas_call(channel_kernel, in_specs=[smem_spec(), any_spec(), any_spe...  26.7 us
    all_to_all x1, waiting for transfers between devices, exchange(): lax.all_to_all(tiles, ('row', 'col'), split_axis=0, concat_axis=0, tiled=...  23 us
    ppermute x1, waiting for transfers between devices, panel_pieces(): same = lax.ppermute(same, ('row', 'col'), route(0))  19.3 us
    pallas_call x1, Pallas kernels, panel_part(): pl.pallas_call(panel_kernel, grid=(N_COL // 2,), in_specs=[pl.BlockSpec((...  14.8 us
    all_to_all x1, starting transfers between devices, exchange(): lax.all_to_all(tiles, ('row', 'col'), split_axis=0, concat_axis=0, tiled=...  11.2 us
    pallas_call x1, Pallas kernels, updates(): pl.pallas_call(send_kernel, in_specs=[smem_spec()] * 5 + [vmem_spec()], o...  8.7 us
  transfers between devices with their start and end apart: 5, of which 4 were waited for; matrix products, arithmetic and copies ran while one was open for 2% of the time, Pallas kernels for 14%

profile of v2, /device:TPU:8, one launch (start us, length us, event | category | flops | bytes accessed | tf_op | source)
XLA Modules:
  0.0 344.2 jit_solution(6796403035528352053)
XLA Ops:
  7.2 0.0 copy-start.1
  7.2 0.0 all-gather.2.cloned.1.call-start
  7.2 1.2 select_reduce_fusion.1
  8.5 1.4 multiply_convert_fusion.1
  9.9 0.1 fusion.2
  10.0 2.8 collective-permute-start
  12.8 0.1 fusion
  12.9 3.5 %collective-permute-start.1 = (bf16[2,768,128]{2,1,0:T(8,128)(2,1)S(1)}, bf16[2,768,128]{2,1,0:T(8,128)(2,1)S(1)}, u32[]{:S(2)}, u32[]{:S(2)}) collective-permute-start(bf16[2,768,128]{2,1,0:T(8,128)(2,1)S(1)} %fusion), channel_id=1, source_target_pairs={{0,0},{1,1},{2,16},{3,17},{4,32},{5,33},{6,48},{7,49},{8,64},{9,65... | collective-permute-start | bytes 1179656 | tf_op jit(solution)/shard_map/ppermute | solution.py:307
  16.3 0.0 copy-done.1
  16.3 0.6 convert_element_type.20.weight_ref
  17.5 8.7 %send.1 = (bf16[128,264,128]{2,1,0:T(8,128)(2,1)}, s32[256]{0:T(256)}, f32[256]{0:T(256)}) custom-call(s32[1]{0:T(128)S(6)} %copy.29.live_ref, s32[1,144]{1,0:T(1,128)} %source_ref.1, s32[1,144]{1,0:T(1,128)} %owner_ref.1, s32[1,144]{1,0:T(1,128)} %place_ref.1, f32[1,144]{1,0:T(1,128)} %convert_element_type.20.weight_ref, bf16[1536,768]{1,0:T(8,128)(2,1)} %eta_ref.3), custom_call_target="tpu_custom_call" | custom-call | bytes 11534336 | tf_op jit(solution)/shard_map/send/pallas_call | solution.py:367
  26.2 2.4 collective-permute-done
  28.7 19.3 %collective-permute-done.1 = bf16[2,768,128]{2,1,0:T(8,128)(2,1)S(1)} collective-permute-done((bf16[2,768,128]{2,1,0:T(8,128)(2,1)S(1)}, bf16[2,768,128]{2,1,0:T(8,128)(2,1)S(1)}, u32[]{:S(2)}, u32[]{:S(2)}) %collective-permute-start.1) | collective-permute-done | bytes 393248 | tf_op jit(solution)/shard_map/ppermute | solution.py:307
  48.0 0.1 select_bitcast_fusion.1
  48.0 0.9 pad_maximum_fusion
  49.0 0.0 all-gather.2.cloned.1.call-update
  49.0 11.2 %all-to-all-start = ((bf16[128,264,128]{2,1,0:T(8,128)(2,1)}), bf16[128,264,128]{2,1,0:T(8,128)(2,1)}, u32[]{:S(2)}, u32[]{:S(2)}) async-start(bf16[128,264,128]{2,1,0:T(8,128)(2,1)} %get-tuple-element.11), calls=%async_computation.1 | async-start | bytes 17301504 | tf_op jit(solution)/shard_map/all_to_all | solution.py:346
  60.2 0.0 reduce-scatter.2.cloned.1.call-start
  60.3 85.8 %all-gather.2.cloned.1.call-done = bf16[24576,128]{1,0:T(8,128)(2,1)} async-done(((bf16[3072,128]{1,0:T(8,128)(2,1)}), bf16[24576,128]{1,0:T(8,128)(2,1)}) %all-gather.2.cloned.1.call-update) | async-done | bytes 6291472 | tf_op jit(solution)/shard_map/all_gather | solution.py:313
  146.1 14.8 %panel.1 = bf16[16,1536,128]{2,1,0:T(8,128)(2,1)} custom-call(bf16[1536,768]{1,0:T(8,128)(2,1)} %eta_ref.3, bf16[1536,768]{1,0:T(8,128)(2,1)} %gamma_ref.1, bf16[16,2,768,128]{3,2,1,0:T(8,128)(2,1)} %bitcast.34), custom_call_target="tpu_custom_call" | custom-call | flops 9663676416 | bytes 20971520 | tf_op jit(solution)/shard_map/panel/pallas_call | solution.py:316
  160.9 0.0 copy-start
  160.9 0.0 reduce-scatter.2.cloned.1.call-update
  160.9 0.7 copy-done
  161.6 1.2 copy.27.scale_ref
  162.8 23.0 %all-to-all-done.got_ref = bf16[128,264,128]{2,1,0:T(8,128)(2,1)} async-done(((bf16[128,264,128]{2,1,0:T(8,128)(2,1)}), bf16[128,264,128]{2,1,0:T(8,128)(2,1)}, u32[]{:S(2)}, u32[]{:S(2)}) %all-to-all-start) | async-done | bytes 8650784 | tf_op jit(solution)/shard_map/all_to_all | solution.py:346
  185.7 1.5 remainder_reduce_fusion
  187.2 0.1 div.10
  187.4 0.1 rem.39
  187.5 1.3 compare_reduce_fusion
  188.8 0.1 ne.34
  189.0 0.6 fusion.4.place_ref
  189.6 26.7 %channel.1 = bf16[128,256,128]{2,1,0:T(8,128)(2,1)} custom-call(s32[256]{0:T(256)} %fusion.4.place_ref, bf16[128,264,128]{2,1,0:T(8,128)(2,1)} %all-to-all-done.got_ref, bf16[1536,1536]{1,0:T(8,128)(2,1)} %bitcast.35, f32[1536,1]{1,0:T(8,128)} %copy.27.scale_ref), custom_call_target="tpu_custom_call" | custom-call | flops 14495514624 | bytes 23068672 | tf_op jit(solution)/shard_map/channel/pallas_call | solution.py:392
  216.2 113.0 %all_to_all.10.back_ref = bf16[128,256,128]{2,1,0:T(8,128)(2,1)} all-to-all(bf16[128,256,128]{2,1,0:T(8,128)(2,1)} %channel.1), channel_id=1, replica_groups=mesh['row'=8,'col'=16] {'row','col'}, dimensions={0} | all-to-all | bytes 16777216 | tf_op jit(solution)/shard_map/all_to_all | solution.py:346
  329.3 6.2 %update.1 = bf16[1536,768]{1,0:T(8,128)(2,1)} custom-call(s32[256]{0:T(256)} %get-tuple-element.9.tile_ref, f32[256]{0:T(256)} %get-tuple-element.10.factor_ref, bf16[128,256,128]{2,1,0:T(8,128)(2,1)} %all_to_all.10.back_ref), custom_call_target="tpu_custom_call" | custom-call | bytes 11534336 | tf_op jit(solution)/shard_map/update/pallas_call | solution.py:414
  335.4 0.0 reduce-scatter.2.cloned.1.call-done.in_ref
  335.5 1.9 turn.1
  (1 shorter events, 0.0 us)
Async XLA Ops:
  7.2 9.2 %copy-start.1 = (bf16[1,144]{1,0:T(2,128)(2,1)S(1)}, bf16[1,144]{1,0:T(2,128)(2,1)}, u32[]{:S(2)}) copy-start(bf16[1,144]{1,0:T(2,128)(2,1)} %param.22) | copy-start | bytes 868
  7.2 138.9 %all-gather.2.cloned.1.call-start = ((), (), s32[]{:S(2)}) async-start(), calls=%async_computation.3 | async-start | bytes 7077888 | tf_op jit(solution)/shard_map/all_gather | solution.py:313
  10.0 18.7 %collective-permute-start = (bf16[2,768,128]{2,1,0:T(8,128)(2,1)S(1)}, bf16[2,768,128]{2,1,0:T(8,128)(2,1)S(1)}, u32[]{:S(2)}, u32[]{:S(2)}) collective-permute-start(bf16[2,768,128]{2,1,0:T(8,128)(2,1)S(1)} %fusion.2), channel_id=1, source_target_pairs={{0,1},{1,0},{2,17},{3,16},{4,33},{5,32},{6,49},{7,48},{8,65},{9,64... | collective-permute-start | bytes 1179656 | tf_op jit(solution)/shard_map/ppermute | solution.py:308
  12.9 35.1 %collective-permute-start.1 = (bf16[2,768,128]{2,1,0:T(8,128)(2,1)S(1)}, bf16[2,768,128]{2,1,0:T(8,128)(2,1)S(1)}, u32[]{:S(2)}, u32[]{:S(2)}) collective-permute-start(bf16[2,768,128]{2,1,0:T(8,128)(2,1)S(1)} %fusion), channel_id=1, source_target_pairs={{0,0},{1,1},{2,16},{3,17},{4,32},{5,33},{6,48},{7,49},{8,64},{9,65... | collective-permute-start | bytes 1179656 | tf_op jit(solution)/shard_map/ppermute | solution.py:307
  49.0 136.7 %all-to-all-start = ((bf16[128,264,128]{2,1,0:T(8,128)(2,1)}), bf16[128,264,128]{2,1,0:T(8,128)(2,1)}, u32[]{:S(2)}, u32[]{:S(2)}) async-start(bf16[128,264,128]{2,1,0:T(8,128)(2,1)} %get-tuple-element.11), calls=%async_computation.1 | async-start | bytes 17301504 | tf_op jit(solution)/shard_map/all_to_all | solution.py:346
  60.2 275.2 %reduce-scatter.2.cloned.1.call-start = ((), (), s32[]{:S(2)}) async-start(), calls=%async_computation.4 | async-start | bytes 6684672 | tf_op jit(solution)/shard_map/reduce_scatter | solution.py:332
  160.9 0.7 copy-start
Sparse Core Ops, SparseCore 0:
  49.1 96.9 all-gather.1
  161.0 166.7 reduce-scatter.1

commit v3 on v2

--- a/solution.py
+++ b/solution.py
@@ -19,6 +19,7 @@
 CAP = 2
 N_ROW = 8
 N_COL = 16
+SIDE = 4
 GROUP = 16
 CODE_ROWS = 8
 VMEM_LIMIT = 60 * 1024 * 1024
@@ -94,7 +95,9 @@
         r = t // COL_TILES
         tile_ref[n] = r * 8 + (t - r * COL_TILES)
         factor_ref[n] = weight_ref[0, s]
-        place_of[n] = place_ref[0, s]
+        u = place_ref[0, s]
+        v = u // PH_TILES
+        place_of[n] = v * 16 + (u - v * PH_TILES)
         return carry
 
     lax.fori_loop(0, live_ref[0], slot, 0)
@@ -263,7 +266,7 @@
     step_through(BLOCKS // GROUP, 1, finish)
 
 
-def panel_kernel(eta_ref, gamma_ref, panel_ref, out_ref):
+def panel_kernel(x_ref, eta_ref, gamma_ref, panel_ref, out_ref):
     gamma_cols = jnp.concatenate([panel_ref[0, 0], panel_ref[1, 0]], axis=1)
     eta_cols = jnp.concatenate([panel_ref[0, 1], panel_ref[1, 1]], axis=1)
     part = jnp.dot(eta_ref[...], gamma_cols, preferred_element_type=f32)
@@ -296,9 +299,12 @@
     def swap(first, second):
         return jnp.where(odd, second, first), jnp.where(odd, first, second)
 
+    def turned(i, c):
+        return 2 * ((i // 2 + c // SIDE) % SIDE) + c % SIDE // 2
+
     def route(flip):
         return [
-            (i * N_COL + c, (c // 2) * N_COL + 2 * i + (c + flip) % 2)
+            (i * N_COL + c, turned(i, c) * N_COL + 2 * i + (c + flip) % 2)
             for i in range(N_ROW)
             for c in range(N_COL)
         ]
@@ -315,20 +321,26 @@
     ).reshape(N_COL, 2, COLS, PANEL_DEV)
     sums = pl.pallas_call(
         panel_kernel,
-        grid=(N_COL // 2,),
-        in_specs=[
-            pl.BlockSpec((ROWS, COLS), lambda c: (0, 0)),
-            pl.BlockSpec((ROWS, COLS), lambda c: (0, 0)),
-            pl.BlockSpec((2, 2, COLS, PANEL_DEV), lambda c: (c, 0, 0, 0)),
-        ],
-        out_specs=pl.BlockSpec((2, ROWS, PANEL_DEV), lambda c: (c, 0, 0)),
+        grid_spec=pltpu.PrefetchScalarGridSpec(
+            num_scalar_prefetch=1,
+            grid=(SIDE, 2),
+            in_specs=[
+                pl.BlockSpec((ROWS, COLS), lambda y, h, x: (0, 0)),
+                pl.BlockSpec((ROWS, COLS), lambda y, h, x: (0, 0)),
+                pl.BlockSpec(
+                    (2, 2, COLS, PANEL_DEV),
+                    lambda y, h, x: (2 * lax.rem(y + x[0], SIDE) + h, 0, 0, 0),
+                ),
+            ],
+            out_specs=pl.BlockSpec((2, ROWS, PANEL_DEV), lambda y, h, x: (2 * y + h, 0, 0)),
+        ),
         out_shape=jax.ShapeDtypeStruct((N_COL, ROWS, PANEL_DEV), bf16),
         compiler_params=params(),
         cost_estimate=pl.CostEstimate(
             flops=4 * ROWS * COLS * N_COL * PANEL_DEV, bytes_accessed=20 << 20, transcendentals=0
         ),
         name="panel",
-    )(eta_pairs, gamma_pairs, whole)
+    )((lax.axis_index("col") // SIDE).reshape(1), eta_pairs, gamma_pairs, whole)
     done = lax.psum_scatter(
         sums.reshape(N_COL * ROWS, PANEL_DEV), "col", scatter_dimension=0, tiled=True
     )
@@ -387,7 +399,6 @@
     panel_update = panel_part(eta_pairs, gamma_pairs, pieces)
     received = exchange(sent)
     places = received[:, rows, :CAP].astype(jnp.int32).reshape(slots)
-    places = places // PH_TILES * 16 + places % PH_TILES
     whole = (PH_STATES, PH_STATES)
     answers = pl.pallas_call(
         channel_kernel,

time: 347 us -> 331 us (0.954)
  waiting for transfers between devices: 131 us -> 115 us
    ppermute x1, waiting for transfers between devices: 19.3 us -> 6.77 us  [panel_pieces(): same = lax.ppermute(same, ('row', 'col'), route(0))]
  transfers between devices with their start and end apart: 5 -> 5, of which waited for: 4 -> 3; matrix products, arithmetic and copies ran while one was open for 2% -> 1% of each run, Pallas kernels for 14% -> 15%
where the time goes in v3:
time: 331 us; the launch traced here: 325 us
  waiting for transfers between devices  115 us (35%)
  blocking collectives  112 us (34%)
  Pallas kernels  57.9 us (17%)
  starting transfers between devices  16.9 us (5%)
  between operations  14.8 us (4%)
  other arithmetic  5.51 us (2%)
    all_to_all x1, blocking collectives, exchange(): lax.all_to_all(tiles, ('row', 'col'), split_axis=0, concat_axis=0, tiled=...  112 us
    all_gather x1, waiting for transfers between devices, panel_part(): lax.all_gather(pieces.reshape(4 * COLS, PANEL_DEV), 'row', axis=0, tiled=...  85.8 us
    pallas_call x1, Pallas kernels, updates(): pl.pallas_call(channel_kernel, in_specs=[smem_spec(), any_spec(), any_spe...  26.6 us
    all_to_all x1, waiting for transfers between devices, exchange(): lax.all_to_all(tiles, ('row', 'col'), split_axis=0, concat_axis=0, tiled=...  22.9 us
    pallas_call x1, Pallas kernels, panel_part(): pl.pallas_call(panel_kernel, grid_spec=pltpu.PrefetchScalarGridSpec(num_s...  14.9 us
    all_to_all x1, starting transfers between devices, exchange(): lax.all_to_all(tiles, ('row', 'col'), split_axis=0, concat_axis=0, tiled=...  10.5 us
    pallas_call x1, Pallas kernels, updates(): pl.pallas_call(send_kernel, in_specs=[smem_spec()] * 5 + [vmem_spec()], o...  8.25 us
    ppermute x1, waiting for transfers between devices, panel_pieces(): same = lax.ppermute(same, ('row', 'col'), route(0))  6.77 us
  transfers between devices with their start and end apart: 5, of which 3 were waited for; matrix products, arithmetic and copies ran while one was open for 1% of the time, Pallas kernels for 15%

profile of v3, /device:TPU:8, one launch (start us, length us, event | category | flops | bytes accessed | tf_op | source)
XLA Modules:
  0.0 324.8 jit_solution(1115920571083650646)
XLA Ops:
  7.2 0.0 copy-start.1
  7.2 0.0 all-gather.2.cloned.1.call-start
  7.2 1.2 select_reduce_fusion.1
  8.5 1.4 multiply_convert_fusion.1
  9.9 0.1 fusion.2
  10.0 2.8 collective-permute-start
  12.8 0.1 fusion
  12.8 3.5 %collective-permute-start.1 = (bf16[2,768,128]{2,1,0:T(8,128)(2,1)S(1)}, bf16[2,768,128]{2,1,0:T(8,128)(2,1)S(1)}, u32[]{:S(2)}, u32[]{:S(2)}) collective-permute-start(bf16[2,768,128]{2,1,0:T(8,128)(2,1)S(1)} %fusion), channel_id=1, source_target_pairs={{0,0},{1,1},{2,16},{3,17},{4,32},{5,33},{6,48},{7,49},{8,64},{9,65... | collective-permute-start | bytes 1179656 | tf_op jit(solution)/shard_map/ppermute | solution.py:313
  16.3 0.0 copy-done.1
  16.3 0.6 convert_element_type.22.weight_ref
  17.6 8.2 %send.1 = (bf16[128,264,128]{2,1,0:T(8,128)(2,1)}, s32[256]{0:T(256)}, f32[256]{0:T(256)}) custom-call(s32[1]{0:T(128)S(6)} %copy.29.live_ref, s32[1,144]{1,0:T(1,128)} %source_ref.1, s32[1,144]{1,0:T(1,128)} %owner_ref.1, s32[1,144]{1,0:T(1,128)} %place_ref.1, f32[1,144]{1,0:T(1,128)} %convert_element_type.22.weight_ref, bf16[1536,768]{1,0:T(8,128)(2,1)} %eta_ref.3), custom_call_target="tpu_custom_call" | custom-call | bytes 11534336 | tf_op jit(solution)/shard_map/send/pallas_call | solution.py:379
  25.8 0.0 collective-permute-done
  25.8 6.8 %collective-permute-done.1 = bf16[2,768,128]{2,1,0:T(8,128)(2,1)S(1)} collective-permute-done((bf16[2,768,128]{2,1,0:T(8,128)(2,1)S(1)}, bf16[2,768,128]{2,1,0:T(8,128)(2,1)S(1)}, u32[]{:S(2)}, u32[]{:S(2)}) %collective-permute-start.1) | collective-permute-done | bytes 393248 | tf_op jit(solution)/shard_map/ppermute | solution.py:313
  32.6 0.1 select_bitcast_fusion.1
  32.7 0.9 pad_maximum_fusion
  33.6 0.0 all-gather.2.cloned.1.call-update
  33.6 10.5 %all-to-all-start = ((bf16[128,264,128]{2,1,0:T(8,128)(2,1)}), bf16[128,264,128]{2,1,0:T(8,128)(2,1)}, u32[]{:S(2)}, u32[]{:S(2)}) async-start(bf16[128,264,128]{2,1,0:T(8,128)(2,1)} %get-tuple-element.11), calls=%async_computation.1 | async-start | bytes 17301504 | tf_op jit(solution)/shard_map/all_to_all | solution.py:358
  44.1 0.0 reduce-scatter.2.cloned.1.call-start
  44.2 85.8 %all-gather.2.cloned.1.call-done = bf16[24576,128]{1,0:T(8,128)(2,1)} async-done(((bf16[3072,128]{1,0:T(8,128)(2,1)}), bf16[24576,128]{1,0:T(8,128)(2,1)}) %all-gather.2.cloned.1.call-update) | async-done | bytes 6291472 | tf_op jit(solution)/shard_map/all_gather | solution.py:319
  130.0 14.9 %panel.1 = bf16[16,1536,128]{2,1,0:T(8,128)(2,1)} custom-call(s32[1]{0:T(128)} %bitcast.x_ref, bf16[1536,768]{1,0:T(8,128)(2,1)} %eta_ref.3, bf16[1536,768]{1,0:T(8,128)(2,1)} %gamma_ref.1, bf16[16,2,768,128]{3,2,1,0:T(8,128)(2,1)} %bitcast.35), custom_call_target="tpu_custom_call" | custom-call | flops 9663676416 | bytes 20971520 | tf_op jit(solution)/shard_map/panel/pallas_call | solution.py:322
  144.9 0.0 copy-start
  144.9 0.0 reduce-scatter.2.cloned.1.call-update
  144.9 0.7 copy-done
  145.6 1.2 copy.27.scale_ref
  146.8 22.9 %all-to-all-done.got_ref = bf16[128,264,128]{2,1,0:T(8,128)(2,1)} async-done(((bf16[128,264,128]{2,1,0:T(8,128)(2,1)}), bf16[128,264,128]{2,1,0:T(8,128)(2,1)}, u32[]{:S(2)}, u32[]{:S(2)}) %all-to-all-start) | async-done | bytes 8650784 | tf_op jit(solution)/shard_map/all_to_all | solution.py:358
  169.6 1.2 fusion.3
  170.8 0.7 reshape.46.place_ref
  171.5 26.6 %channel.1 = bf16[128,256,128]{2,1,0:T(8,128)(2,1)} custom-call(s32[256]{0:T(256)} %reshape.46.place_ref, bf16[128,264,128]{2,1,0:T(8,128)(2,1)} %all-to-all-done.got_ref, bf16[1536,1536]{1,0:T(8,128)(2,1)} %bitcast.36, f32[1536,1]{1,0:T(8,128)} %copy.27.scale_ref), custom_call_target="tpu_custom_call" | custom-call | flops 14495514624 | bytes 23068672 | tf_op jit(solution)/shard_map/channel/pallas_call | solution.py:403
  198.1 111.7 %all_to_all.10.back_ref = bf16[128,256,128]{2,1,0:T(8,128)(2,1)} all-to-all(bf16[128,256,128]{2,1,0:T(8,128)(2,1)} %channel.1), channel_id=1, replica_groups=mesh['row'=8,'col'=16] {'row','col'}, dimensions={0} | all-to-all | bytes 16777216 | tf_op jit(solution)/shard_map/all_to_all | solution.py:358
  309.8 6.2 %update.1 = bf16[1536,768]{1,0:T(8,128)(2,1)} custom-call(s32[256]{0:T(256)} %get-tuple-element.9.tile_ref, f32[256]{0:T(256)} %get-tuple-element.10.factor_ref, bf16[128,256,128]{2,1,0:T(8,128)(2,1)} %all_to_all.10.back_ref), custom_call_target="tpu_custom_call" | custom-call | bytes 11534336 | tf_op jit(solution)/shard_map/update/pallas_call | solution.py:425
  316.0 0.0 reduce-scatter.2.cloned.1.call-done.in_ref
  316.1 1.9 turn.1
  (1 shorter events, 0.0 us)
Async XLA Ops:
  7.2 9.2 %copy-start.1 = (bf16[1,144]{1,0:T(2,128)(2,1)S(1)}, bf16[1,144]{1,0:T(2,128)(2,1)}, u32[]{:S(2)}) copy-start(bf16[1,144]{1,0:T(2,128)(2,1)} %param.22) | copy-start | bytes 868
  7.2 122.8 %all-gather.2.cloned.1.call-start = ((), (), s32[]{:S(2)}) async-start(), calls=%async_computation.3 | async-start | bytes 7077888 | tf_op jit(solution)/shard_map/all_gather | solution.py:319
  10.0 15.8 %collective-permute-start = (bf16[2,768,128]{2,1,0:T(8,128)(2,1)S(1)}, bf16[2,768,128]{2,1,0:T(8,128)(2,1)S(1)}, u32[]{:S(2)}, u32[]{:S(2)}) collective-permute-start(bf16[2,768,128]{2,1,0:T(8,128)(2,1)S(1)} %fusion.2), channel_id=1, source_target_pairs={{0,1},{1,0},{2,17},{3,16},{4,33},{5,32},{6,49},{7,48},{8,65},{9,64... | collective-permute-start | bytes 1179656 | tf_op jit(solution)/shard_map/ppermute | solution.py:314
  12.8 19.8 %collective-permute-start.1 = (bf16[2,768,128]{2,1,0:T(8,128)(2,1)S(1)}, bf16[2,768,128]{2,1,0:T(8,128)(2,1)S(1)}, u32[]{:S(2)}, u32[]{:S(2)}) collective-permute-start(bf16[2,768,128]{2,1,0:T(8,128)(2,1)S(1)} %fusion), channel_id=1, source_target_pairs={{0,0},{1,1},{2,16},{3,17},{4,32},{5,33},{6,48},{7,49},{8,64},{9,65... | collective-permute-start | bytes 1179656 | tf_op jit(solution)/shard_map/ppermute | solution.py:313
  33.6 136.0 %all-to-all-start = ((bf16[128,264,128]{2,1,0:T(8,128)(2,1)}), bf16[128,264,128]{2,1,0:T(8,128)(2,1)}, u32[]{:S(2)}, u32[]{:S(2)}) async-start(bf16[128,264,128]{2,1,0:T(8,128)(2,1)} %get-tuple-element.11), calls=%async_computation.1 | async-start | bytes 17301504 | tf_op jit(solution)/shard_map/all_to_all | solution.py:358
  44.1 271.9 %reduce-scatter.2.cloned.1.call-start = ((), (), s32[]{:S(2)}) async-start(), calls=%async_computation.4 | async-start | bytes 6684672 | tf_op jit(solution)/shard_map/reduce_scatter | solution.py:344
  144.9 0.7 copy-start
Sparse Core Ops, SparseCore 0:
  33.8 96.1 all-gather.1
  145.1 166.5 reduce-scatter.1

commit v4 on v3

--- a/solution.py
+++ b/solution.py
@@ -65,15 +65,20 @@
     owner_ref,
     place_ref,
     weight_ref,
-    eta_ref,
+    eta_hbm,
     out_ref,
     tile_ref,
     factor_ref,
     place_of,
     counts,
     held,
+    eta_ref,
     sems,
+    eta_sem,
 ):
+    eta_copy = pltpu.make_async_copy(eta_hbm, eta_ref, eta_sem)
+    eta_copy.start()
+
     def clear(n):
         tile_ref[n] = 0
         factor_ref[n] = 0.0
@@ -102,6 +107,7 @@
 
     lax.fori_loop(0, live_ref[0], slot, 0)
     lane = lax.broadcasted_iota(jnp.int32, (CODE_ROWS, TILE), 1)
+    eta_copy.wait()
 
     def copy(j):
         part = pl.ds(j * GROUP, GROUP)
@@ -132,7 +138,9 @@
     step_through(BLOCKS // GROUP, 1, finish)
 
 
-def update_kernel(tile_ref, factor_ref, back_ref, out_ref, held, total, sems):
+def update_kernel(
+    tile_ref, factor_ref, back_ref, sums_ref, out_ref, turned_ref, held, total, other, sems
+):
     def copy(j):
         part = pl.ds(j * GROUP, GROUP)
         return pltpu.make_async_copy(back_ref.at[part], held.at[part], sems.at[j])
@@ -144,19 +152,21 @@
 
     def clear(r):
         total[aligned(r, TILE), :] = jnp.zeros((TILE, COLS), f32)
+        other[aligned(r, TILE), :] = jnp.zeros((TILE, COLS), f32)
 
     step_through(ROWS // TILE, 1, clear)
+    turned_ref[...] = sums_ref[...].astype(f32).T.astype(bf16)
 
     def group(j, carry):
         copy(j).wait()
 
         def owner(i):
             q = j * GROUP + i
-            for k in range(CAP):
+            for k, into in enumerate((total, other)):
                 n = q * CAP + k
                 t = tile_ref[n]
                 rows, cols = aligned(t >> 3, TILE), aligned(t & 7, TILE)
-                total[rows, cols] += factor_ref[n] * held[
+                into[rows, cols] += factor_ref[n] * held[
                     q, k * TILE : (k + 1) * TILE, :
                 ].astype(f32)
 
@@ -167,7 +177,7 @@
 
     def finish(r):
         rows = aligned(r, TILE)
-        out_ref[rows, :] = total[rows, :].astype(bf16)
+        out_ref[rows, :] = (total[rows, :] + other[rows, :]).astype(bf16)
 
     step_through(ROWS // TILE, 1, finish)
 
@@ -267,17 +277,13 @@
 
 
 def panel_kernel(x_ref, eta_ref, gamma_ref, panel_ref, out_ref):
-    gamma_cols = jnp.concatenate([panel_ref[0, 0], panel_ref[1, 0]], axis=1)
-    eta_cols = jnp.concatenate([panel_ref[0, 1], panel_ref[1, 1]], axis=1)
+    gamma_cols = jnp.concatenate([panel_ref[k, 0] for k in range(SIDE)], axis=1)
+    eta_cols = jnp.concatenate([panel_ref[k, 1] for k in range(SIDE)], axis=1)
     part = jnp.dot(eta_ref[...], gamma_cols, preferred_element_type=f32)
     part -= jnp.dot(gamma_ref[...], eta_cols, preferred_element_type=f32)
     part = part.astype(bf16)
-    for k in range(2):
+    for k in range(SIDE):
         out_ref[k] = part[:, k * PANEL_DEV : (k + 1) * PANEL_DEV]
-
-
-def turn_kernel(in_ref, out_ref):
-    out_ref[...] = in_ref[...].astype(f32).T.astype(bf16)
 
 
 def orbit_lookup(pair_ids, occupancy):
@@ -299,12 +305,13 @@
     def swap(first, second):
         return jnp.where(odd, second, first), jnp.where(odd, first, second)
 
-    def turned(i, c):
-        return 2 * ((i // 2 + c // SIDE) % SIDE) + c % SIDE // 2
+    def target(i, c, h):
+        x = (i // 2 + c // SIDE + i % 2 + 2 * h) % SIDE
+        return (2 * x + c % SIDE // 2) * N_COL + 2 * i + h
 
     def route(flip):
         return [
-            (i * N_COL + c, turned(i, c) * N_COL + 2 * i + (c + flip) % 2)
+            (i * N_COL + c, target(i, c, (c + flip) % 2))
             for i in range(N_ROW)
             for c in range(N_COL)
         ]
@@ -319,20 +326,22 @@
     whole = lax.all_gather(
         pieces.reshape(4 * COLS, PANEL_DEV), "row", axis=0, tiled=True
     ).reshape(N_COL, 2, COLS, PANEL_DEV)
+    me = lax.axis_index("col")
+    turn = me // SIDE + me // 2 % 2 + me % 2 * 2
     sums = pl.pallas_call(
         panel_kernel,
         grid_spec=pltpu.PrefetchScalarGridSpec(
             num_scalar_prefetch=1,
-            grid=(SIDE, 2),
+            grid=(SIDE,),
             in_specs=[
-                pl.BlockSpec((ROWS, COLS), lambda y, h, x: (0, 0)),
-                pl.BlockSpec((ROWS, COLS), lambda y, h, x: (0, 0)),
+                pl.BlockSpec((ROWS, COLS), lambda y, x: (0, 0)),
+                pl.BlockSpec((ROWS, COLS), lambda y, x: (0, 0)),
                 pl.BlockSpec(
-                    (2, 2, COLS, PANEL_DEV),
-                    lambda y, h, x: (2 * lax.rem(y + x[0], SIDE) + h, 0, 0, 0),
+                    (SIDE, 2, COLS, PANEL_DEV),
+                    lambda y, x: (lax.rem(y + x[0], SIDE), 0, 0, 0),
                 ),
             ],
-            out_specs=pl.BlockSpec((2, ROWS, PANEL_DEV), lambda y, h, x: (2 * y + h, 0, 0)),
+            out_specs=pl.BlockSpec((SIDE, ROWS, PANEL_DEV), lambda y, x: (y, 0, 0)),
         ),
         out_shape=jax.ShapeDtypeStruct((N_COL, ROWS, PANEL_DEV), bf16),
         compiler_params=params(),
@@ -340,18 +349,10 @@
             flops=4 * ROWS * COLS * N_COL * PANEL_DEV, bytes_accessed=20 << 20, transcendentals=0
         ),
         name="panel",
-    )((lax.axis_index("col") // SIDE).reshape(1), eta_pairs, gamma_pairs, whole)
-    done = lax.psum_scatter(
+    )(turn.reshape(1), eta_pairs, gamma_pairs, whole)
+    return lax.psum_scatter(
         sums.reshape(N_COL * ROWS, PANEL_DEV), "col", scatter_dimension=0, tiled=True
     )
-    return pl.pallas_call(
-        turn_kernel,
-        in_specs=[vmem_spec()],
-        out_specs=vmem_spec(),
-        out_shape=jax.ShapeDtypeStruct((PANEL_DEV, ROWS), bf16),
-        compiler_params=params(),
-        name="turn",
-    )(done)
 
 
 def exchange(tiles):
@@ -378,7 +379,7 @@
     held = pltpu.VMEM((BLOCKS, rows, TILE), bf16)
     sent, tiles, factors = pl.pallas_call(
         send_kernel,
-        in_specs=[smem_spec()] * 5 + [vmem_spec()],
+        in_specs=[smem_spec()] * 5 + [any_spec()],
         out_specs=[any_spec(), smem_spec(), smem_spec()],
         out_shape=[
             jax.ShapeDtypeStruct((BLOCKS, rows + CODE_ROWS, TILE), bf16),
@@ -389,14 +390,16 @@
             pltpu.SMEM((slots,), jnp.int32),
             pltpu.SMEM((BLOCKS,), jnp.int32),
             pltpu.VMEM((BLOCKS, rows + CODE_ROWS, TILE), bf16),
+            pltpu.VMEM((ROWS, COLS), bf16),
             dma((groups,)),
+            dma,
         ],
         compiler_params=params(),
         cost_estimate=pl.CostEstimate(flops=0, bytes_accessed=11 << 20, transcendentals=0),
         name="send",
     )(live_count, tile_source, tile_owner, tile_place, weights, eta_pairs)
     sent, pieces = lax.optimization_barrier((sent, pieces))
-    panel_update = panel_part(eta_pairs, gamma_pairs, pieces)
+    panel_sums = panel_part(eta_pairs, gamma_pairs, pieces)
     received = exchange(sent)
     places = received[:, rows, :CAP].astype(jnp.int32).reshape(slots)
     whole = (PH_STATES, PH_STATES)
@@ -422,16 +425,19 @@
         name="channel",
     )(places, received, gamma_recoupled[0], ph_factor.reshape(PH_STATES, 1))
     returned = exchange(answers)
-    recoupled_update = pl.pallas_call(
+    recoupled_update, panel_update = pl.pallas_call(
         update_kernel,
-        in_specs=[smem_spec(), smem_spec(), any_spec()],
-        out_specs=vmem_spec(),
-        out_shape=jax.ShapeDtypeStruct((ROWS, COLS), bf16),
-        scratch_shapes=[held, pltpu.VMEM((ROWS, COLS), f32), dma((groups,))],
+        in_specs=[smem_spec(), smem_spec(), any_spec(), vmem_spec()],
+        out_specs=[vmem_spec(), vmem_spec()],
+        out_shape=[
+            jax.ShapeDtypeStruct((ROWS, COLS), bf16),
+            jax.ShapeDtypeStruct((PANEL_DEV, ROWS), bf16),
+        ],
+        scratch_shapes=[held] + [pltpu.VMEM((ROWS, COLS), f32)] * 2 + [dma((groups,))],
         compiler_params=params(),
         cost_estimate=pl.CostEstimate(flops=0, bytes_accessed=11 << 20, transcendentals=0),
         name="update",
-    )(tiles, factors, returned)
+    )(tiles, factors, returned, panel_sums)
     return (panel_update, recoupled_update)
 
 

time: 331 us -> 324 us (0.979)
  waiting for transfers between devices: 115 us -> 111 us
    ppermute x1, waiting for transfers between devices: 6.77 us -> 1.97 us  [panel_pieces(): same = lax.ppermute(same, ('row', 'col'), route(0))]
    pallas_call x2 -> x1, Pallas kernels: 10.2 us -> 8.36 us  [updates(): pl.pallas_call(send_kernel, in_specs=[smem_spec()] * 5 + [any_spec()], ou...]
  transfers between devices with their start and end apart: 5 -> 5, of which waited for: 3 -> 4; matrix products, arithmetic and copies ran while one was open for 1% -> 1% of each run, Pallas kernels for 15% -> 13%
where the time goes in v4:
time: 324 us; the launch traced here: 321 us
  blocking collectives  112 us (35%)
  waiting for transfers between devices  111 us (34%)
  Pallas kernels  56.4 us (17%)
  starting transfers between devices  18.2 us (6%)
  between operations  14.9 us (5%)
  other arithmetic  5.51 us (2%)
    all_to_all x1, blocking collectives, exchange(): lax.all_to_all(tiles, ('row', 'col'), split_axis=0, concat_axis=0, tiled=...  112 us
    all_gather x1, waiting for transfers between devices, panel_part(): lax.all_gather(pieces.reshape(4 * COLS, PANEL_DEV), 'row', axis=0, tiled=...  85.8 us
    pallas_call x1, Pallas kernels, updates(): pl.pallas_call(channel_kernel, in_specs=[smem_spec(), any_spec(), any_spe...  26.7 us
    all_to_all x1, waiting for transfers between devices, exchange(): lax.all_to_all(tiles, ('row', 'col'), split_axis=0, concat_axis=0, tiled=...  23.2 us
    pallas_call x1, Pallas kernels, panel_part(): pl.pallas_call(panel_kernel, grid_spec=pltpu.PrefetchScalarGridSpec(num_s...  14.6 us
    all_to_all x1, starting transfers between devices, exchange(): lax.all_to_all(tiles, ('row', 'col'), split_axis=0, concat_axis=0, tiled=...  10.3 us
    pallas_call x1, Pallas kernels, updates(): pl.pallas_call(send_kernel, in_specs=[smem_spec()] * 5 + [any_spec()], ou...  8.36 us
    pallas_call x1, Pallas kernels, updates(): pl.pallas_call(update_kernel, in_specs=[smem_spec(), smem_spec(), any_spe...  6.75 us
  transfers between devices with their start and end apart: 5, of which 4 were waited for; matrix products, arithmetic and copies ran while one was open for 1% of the time, Pallas kernels for 13%

profile of v4, /device:TPU:8, one launch (start us, length us, event | category | flops | bytes accessed | tf_op | source)
XLA Modules:
  0.0 320.6 jit_solution(6575223144146891148)
XLA Ops:
  7.2 0.0 copy-start.1
  7.2 0.0 all-gather.2.cloned.1.call-start
  7.2 1.2 select_reduce_fusion.1
  8.5 1.4 multiply_convert_fusion.1
  9.9 0.1 fusion.2
  10.0 4.1 %collective-permute-start = (bf16[2,768,128]{2,1,0:T(8,128)(2,1)S(1)}, bf16[2,768,128]{2,1,0:T(8,128)(2,1)S(1)}, u32[]{:S(2)}, u32[]{:S(2)}) collective-permute-start(bf16[2,768,128]{2,1,0:T(8,128)(2,1)S(1)} %fusion.2), channel_id=1, source_target_pairs={{0,65},{1,0},{2,81},{3,16},{4,97},{5,32},{6,113},{7,48},{8,1},{9,6... | collective-permute-start | bytes 1179656 | tf_op jit(solution)/shard_map/ppermute | solution.py:321
  14.0 0.1 fusion
  14.1 3.8 %collective-permute-start.1 = (bf16[2,768,128]{2,1,0:T(8,128)(2,1)S(1)}, bf16[2,768,128]{2,1,0:T(8,128)(2,1)S(1)}, u32[]{:S(2)}, u32[]{:S(2)}) collective-permute-start(bf16[2,768,128]{2,1,0:T(8,128)(2,1)S(1)} %fusion), channel_id=1, source_target_pairs={{0,0},{1,65},{2,16},{3,81},{4,32},{5,97},{6,48},{7,113},{8,64},{9,... | collective-permute-start | bytes 1179656 | tf_op jit(solution)/shard_map/ppermute | solution.py:320
  18.5 0.0 copy-done.1
  18.6 0.6 convert_element_type.22.weight_ref
  19.1 8.4 %send.1 = (bf16[128,264,128]{2,1,0:T(8,128)(2,1)}, s32[256]{0:T(256)}, f32[256]{0:T(256)}) custom-call(s32[1]{0:T(128)S(6)} %copy.29.live_ref, s32[1,144]{1,0:T(1,128)} %source_ref.1, s32[1,144]{1,0:T(1,128)} %owner_ref.1, s32[1,144]{1,0:T(1,128)} %place_ref.1, f32[1,144]{1,0:T(1,128)} %convert_element_type.22.weight_ref, bf16[1536,768]{1,0:T(8,128)(2,1)} %eta_ref.1), custom_call_target="tpu_custom_call" | custom-call | bytes 11534336 | tf_op jit(solution)/shard_map/send/pallas_call | solution.py:380
  27.5 0.0 collective-permute-done
  27.5 2.0 collective-permute-done.1
  29.5 0.1 select_bitcast_fusion.1
  29.5 0.9 pad_maximum_fusion
  30.5 0.0 all-gather.2.cloned.1.call-update
  30.5 10.3 %all-to-all-start = ((bf16[128,264,128]{2,1,0:T(8,128)(2,1)}), bf16[128,264,128]{2,1,0:T(8,128)(2,1)}, u32[]{:S(2)}, u32[]{:S(2)}) async-start(bf16[128,264,128]{2,1,0:T(8,128)(2,1)} %get-tuple-element.12), calls=%async_computation | async-start | bytes 17301504 | tf_op jit(solution)/shard_map/all_to_all | solution.py:359
  40.8 0.0 reduce-scatter.2.cloned.1.call-start
  40.9 85.8 %all-gather.2.cloned.1.call-done = bf16[24576,128]{1,0:T(8,128)(2,1)} async-done(((bf16[3072,128]{1,0:T(8,128)(2,1)}), bf16[24576,128]{1,0:T(8,128)(2,1)}) %all-gather.2.cloned.1.call-update) | async-done | bytes 6291472 | tf_op jit(solution)/shard_map/all_gather | solution.py:326
  126.6 14.6 %panel.1 = bf16[16,1536,128]{2,1,0:T(8,128)(2,1)} custom-call(s32[1]{0:T(128)} %bitcast.11.x_ref, bf16[1536,768]{1,0:T(8,128)(2,1)} %eta_ref.1, bf16[1536,768]{1,0:T(8,128)(2,1)} %gamma_ref.1, bf16[16,2,768,128]{3,2,1,0:T(8,128)(2,1)} %bitcast.35), custom_call_target="tpu_custom_call" | custom-call | flops 9663676416 | bytes 20971520 | tf_op jit(solution)/shard_map/panel/pallas_call | solution.py:331
  141.2 0.0 copy-start
  141.2 0.0 reduce-scatter.2.cloned.1.call-update
  141.3 0.7 copy-done
  141.9 1.2 copy.27.scale_ref
  143.1 23.2 %all-to-all-done.got_ref = bf16[128,264,128]{2,1,0:T(8,128)(2,1)} async-done(((bf16[128,264,128]{2,1,0:T(8,128)(2,1)}), bf16[128,264,128]{2,1,0:T(8,128)(2,1)}, u32[]{:S(2)}, u32[]{:S(2)}) %all-to-all-start) | async-done | bytes 8650784 | tf_op jit(solution)/shard_map/all_to_all | solution.py:359
  166.3 1.2 fusion.3
  167.5 0.7 reshape.46.place_ref
  168.2 26.7 %channel.1 = bf16[128,256,128]{2,1,0:T(8,128)(2,1)} custom-call(s32[256]{0:T(256)} %reshape.46.place_ref, bf16[128,264,128]{2,1,0:T(8,128)(2,1)} %all-to-all-done.got_ref, bf16[1536,1536]{1,0:T(8,128)(2,1)} %bitcast.36, f32[1536,1]{1,0:T(8,128)} %copy.27.scale_ref), custom_call_target="tpu_custom_call" | custom-call | flops 14495514624 | bytes 23068672 | tf_op jit(solution)/shard_map/channel/pallas_call | solution.py:406
  194.8 111.7 %all_to_all.10.back_ref = bf16[128,256,128]{2,1,0:T(8,128)(2,1)} all-to-all(bf16[128,256,128]{2,1,0:T(8,128)(2,1)} %channel.1), channel_id=1, replica_groups=mesh['row'=8,'col'=16] {'row','col'}, dimensions={0} | all-to-all | bytes 16777216 | tf_op jit(solution)/shard_map/all_to_all | solution.py:359
  306.6 0.4 reduce-scatter.2.cloned.1.call-done.sums_ref
  307.0 6.7 %update.1 = (bf16[1536,768]{1,0:T(8,128)(2,1)}, bf16[128,1536]{1,0:T(8,128)(2,1)}) custom-call(s32[256]{0:T(256)} %get-tuple-element.9.tile_ref, f32[256]{0:T(256)} %get-tuple-element.10.factor_ref, bf16[128,256,128]{2,1,0:T(8,128)(2,1)} %all_to_all.10.back_ref, bf16[1536,128]{1,0:T(8,128)(2,1)} %reduce-scatter.2.cloned.1.call-done.sums_ref), custom_call_target="tpu_custom_call" | custom-call | bytes 11534336 | tf_op jit(solution)/shard_map/update/pallas_call | solution.py:428
  (1 shorter events, 0.0 us)
Async XLA Ops:
  7.2 11.4 %copy-start.1 = (bf16[1,144]{1,0:T(2,128)(2,1)S(1)}, bf16[1,144]{1,0:T(2,128)(2,1)}, u32[]{:S(2)}) copy-start(bf16[1,144]{1,0:T(2,128)(2,1)} %param.22) | copy-start | bytes 868
  7.2 119.5 %all-gather.2.cloned.1.call-start = ((), (), s32[]{:S(2)}) async-start(), calls=%async_computation.3 | async-start | bytes 7077888 | tf_op jit(solution)/shard_map/all_gather | solution.py:326
  10.0 17.5 %collective-permute-start = (bf16[2,768,128]{2,1,0:T(8,128)(2,1)S(1)}, bf16[2,768,128]{2,1,0:T(8,128)(2,1)S(1)}, u32[]{:S(2)}, u32[]{:S(2)}) collective-permute-start(bf16[2,768,128]{2,1,0:T(8,128)(2,1)S(1)} %fusion.2), channel_id=1, source_target_pairs={{0,65},{1,0},{2,81},{3,16},{4,97},{5,32},{6,113},{7,48},{8,1},{9,6... | collective-permute-start | bytes 1179656 | tf_op jit(solution)/shard_map/ppermute | solution.py:321
  14.1 15.4 %collective-permute-start.1 = (bf16[2,768,128]{2,1,0:T(8,128)(2,1)S(1)}, bf16[2,768,128]{2,1,0:T(8,128)(2,1)S(1)}, u32[]{:S(2)}, u32[]{:S(2)}) collective-permute-start(bf16[2,768,128]{2,1,0:T(8,128)(2,1)S(1)} %fusion), channel_id=1, source_target_pairs={{0,0},{1,65},{2,16},{3,81},{4,32},{5,97},{6,48},{7,113},{8,64},{9,... | collective-permute-start | bytes 1179656 | tf_op jit(solution)/shard_map/ppermute | solution.py:320
  30.5 135.8 %all-to-all-start = ((bf16[128,264,128]{2,1,0:T(8,128)(2,1)}), bf16[128,264,128]{2,1,0:T(8,128)(2,1)}, u32[]{:S(2)}, u32[]{:S(2)}) async-start(bf16[128,264,128]{2,1,0:T(8,128)(2,1)} %get-tuple-element.12), calls=%async_computation | async-start | bytes 17301504 | tf_op jit(solution)/shard_map/all_to_all | solution.py:359
  40.8 266.2 %reduce-scatter.2.cloned.1.call-start = ((), (), s32[]{:S(2)}) async-start(), calls=%async_computation.4 | async-start | bytes 6684672 | tf_op jit(solution)/shard_map/reduce_scatter | solution.py:353
  141.2 0.7 copy-start
Sparse Core Ops, SparseCore 0:
  30.6 95.9 all-gather.1
  141.4 165.5 reduce-scatter.1

commit v5 on v4

--- a/solution.py
+++ b/solution.py
@@ -183,7 +183,6 @@
 
 
 def channel_kernel(
-    place_ref,
     got_ref,
     gamma_hbm,
     scale_ref,
@@ -193,10 +192,19 @@
     total,
     eta,
     product,
+    code_rows,
+    codes,
+    place_ref,
     got_sems,
     gamma_sem,
     out_sems,
+    code_sem,
 ):
+    code_copy = pltpu.make_async_copy(
+        got_ref.at[:, pl.ds(CAP * TILE, CODE_ROWS)], code_rows, code_sem
+    )
+    code_copy.start()
+
     def copy(j):
         part = pl.ds(j * GROUP, GROUP)
         return pltpu.make_async_copy(
@@ -210,14 +218,19 @@
 
     step_through(BLOCKS // GROUP, 1, begin)
     gamma_copy.start()
+    code_copy.wait()
+    codes[...] = code_rows[:, 0, :].astype(f32).astype(jnp.int32)
+    place_copy = pltpu.make_async_copy(codes, place_ref, code_sem)
+    place_copy.start()
 
     def clear(r):
         total[aligned(r, TILE), :] = jnp.zeros((TILE, PH_STATES), f32)
 
     step_through(PH_TILES, 1, clear)
-
-    def place(n):
-        code = place_ref[n]
+    place_copy.wait()
+
+    def place(b, k):
+        code = place_ref[b, k]
         return aligned(code >> 4, TILE), aligned(code & 15, TILE)
 
     def group(j, carry):
@@ -226,7 +239,7 @@
         def block(i):
             b = j * GROUP + i
             for k in range(CAP):
-                rows, cols = place(b * CAP + k)
+                rows, cols = place(b, k)
                 total[rows, cols] += held[b, k * TILE : (k + 1) * TILE, :].astype(f32)
 
         step_through(GROUP, 4, block)
@@ -240,7 +253,7 @@
 
     step_through(PH_TILES, 1, settle)
     gamma_copy.wait()
-    width = 256
+    width = 768
 
     def multiply(c):
         cols = aligned(c, width)
@@ -261,7 +274,7 @@
         def block(i):
             b = j * GROUP + i
             for k in range(CAP):
-                rows, cols = place(b * CAP + k)
+                rows, cols = place(b, k)
                 held[b, k * TILE : (k + 1) * TILE, :] = product[rows, cols]
 
         step_through(GROUP, 4, block)
@@ -401,11 +414,10 @@
     sent, pieces = lax.optimization_barrier((sent, pieces))
     panel_sums = panel_part(eta_pairs, gamma_pairs, pieces)
     received = exchange(sent)
-    places = received[:, rows, :CAP].astype(jnp.int32).reshape(slots)
     whole = (PH_STATES, PH_STATES)
     answers = pl.pallas_call(
         channel_kernel,
-        in_specs=[smem_spec(), any_spec(), any_spec(), vmem_spec()],
+        in_specs=[any_spec(), any_spec(), vmem_spec()],
         out_specs=any_spec(),
         out_shape=jax.ShapeDtypeStruct((BLOCKS, rows, TILE), bf16),
         scratch_shapes=[
@@ -414,16 +426,20 @@
             pltpu.VMEM(whole, f32),
             pltpu.VMEM(whole, bf16),
             pltpu.VMEM(whole, bf16),
+            pltpu.VMEM((BLOCKS, CODE_ROWS, TILE), bf16),
+            pltpu.VMEM((BLOCKS, TILE), jnp.int32),
+            pltpu.SMEM((BLOCKS, TILE), jnp.int32),
             dma((groups,)),
             dma,
             dma((groups,)),
+            dma,
         ],
         compiler_params=params(),
         cost_estimate=pl.CostEstimate(
             flops=4 * PH_STATES**3, bytes_accessed=22 << 20, transcendentals=0
         ),
         name="channel",
-    )(places, received, gamma_recoupled[0], ph_factor.reshape(PH_STATES, 1))
+    )(received, gamma_recoupled[0], ph_factor.reshape(PH_STATES, 1))
     returned = exchange(answers)
     recoupled_update, panel_update = pl.pallas_call(
         update_kernel,

time: 324 us -> 324 us (level)
  waiting for transfers between devices: 111 us -> 115 us
where the time goes in v5:
time: 324 us; the launch traced here: 322 us
  waiting for transfers between devices  115 us (35%)
  blocking collectives  111 us (34%)
  Pallas kernels  56 us (17%)
  starting transfers between devices  18.4 us (6%)
  between operations  14.9 us (5%)
  other arithmetic  4.34 us (1%)
    all_to_all x1, blocking collectives, exchange(): lax.all_to_all(tiles, ('row', 'col'), split_axis=0, concat_axis=0, tiled=...  111 us
    all_gather x1, waiting for transfers between devices, panel_part(): lax.all_gather(pieces.reshape(4 * COLS, PANEL_DEV), 'row', axis=0, tiled=...  85.6 us
    pallas_call x1, Pallas kernels, updates(): pl.pallas_call(channel_kernel, in_specs=[any_spec(), any_spec(), vmem_spe...  26.8 us
    all_to_all x1, waiting for transfers between devices, exchange(): lax.all_to_all(tiles, ('row', 'col'), split_axis=0, concat_axis=0, tiled=...  23.2 us
    pallas_call x1, Pallas kernels, panel_part(): pl.pallas_call(panel_kernel, grid_spec=pltpu.PrefetchScalarGridSpec(num_s...  14.6 us
    all_to_all x1, starting transfers between devices, exchange(): lax.all_to_all(tiles, ('row', 'col'), split_axis=0, concat_axis=0, tiled=...  10.3 us
    pallas_call x1, Pallas kernels, updates(): pl.pallas_call(send_kernel, in_specs=[smem_spec()] * 5 + [any_spec()], ou...  7.86 us
    pallas_call x1, Pallas kernels, updates(): pl.pallas_call(update_kernel, in_specs=[smem_spec(), smem_spec(), any_spe...  6.75 us
  transfers between devices with their start and end apart: 5, of which 4 were waited for; matrix products, arithmetic and copies ran while one was open for 1% of the time, Pallas kernels for 13%

profile of v5, /device:TPU:8, one launch (start us, length us, event | category | flops | bytes accessed | tf_op | source)
XLA Modules:
  0.0 321.5 jit_solution(13920797994126396473)
XLA Ops:
  7.2 0.0 copy-start.1
  7.2 0.0 all-gather.2.cloned.1.call-start
  7.2 1.2 select_reduce_fusion.1
  8.5 1.4 multiply_convert_fusion.1
  9.9 0.1 fusion.2
  10.0 4.1 %collective-permute-start = (bf16[2,768,128]{2,1,0:T(8,128)(2,1)S(1)}, bf16[2,768,128]{2,1,0:T(8,128)(2,1)S(1)}, u32[]{:S(2)}, u32[]{:S(2)}) collective-permute-start(bf16[2,768,128]{2,1,0:T(8,128)(2,1)S(1)} %fusion.2), channel_id=1, source_target_pairs={{0,65},{1,0},{2,81},{3,16},{4,97},{5,32},{6,113},{7,48},{8,1},{9,6... | collective-permute-start | bytes 1179656 | tf_op jit(solution)/shard_map/ppermute | solution.py:334
  14.0 0.1 fusion
  14.1 3.8 %collective-permute-start.1 = (bf16[2,768,128]{2,1,0:T(8,128)(2,1)S(1)}, bf16[2,768,128]{2,1,0:T(8,128)(2,1)S(1)}, u32[]{:S(2)}, u32[]{:S(2)}) collective-permute-start(bf16[2,768,128]{2,1,0:T(8,128)(2,1)S(1)} %fusion), channel_id=1, source_target_pairs={{0,0},{1,65},{2,16},{3,81},{4,32},{5,97},{6,48},{7,113},{8,64},{9,... | collective-permute-start | bytes 1179656 | tf_op jit(solution)/shard_map/ppermute | solution.py:333
  18.5 0.0 copy-done.1
  18.6 0.6 convert_element_type.15.weight_ref
  19.1 7.9 %send.1 = (bf16[128,264,128]{2,1,0:T(8,128)(2,1)}, s32[256]{0:T(256)}, f32[256]{0:T(256)}) custom-call(s32[1]{0:T(128)S(6)} %copy.29.live_ref, s32[1,144]{1,0:T(1,128)} %source_ref.1, s32[1,144]{1,0:T(1,128)} %owner_ref.1, s32[1,144]{1,0:T(1,128)} %place_ref.1, f32[1,144]{1,0:T(1,128)} %convert_element_type.15.weight_ref, bf16[1536,768]{1,0:T(8,128)(2,1)} %eta_ref.1), custom_call_target="tpu_custom_call" | custom-call | bytes 11534336 | tf_op jit(solution)/shard_map/send/pallas_call | solution.py:393
  27.0 0.0 collective-permute-done
  27.0 2.5 collective-permute-done.1
  29.5 0.1 select_bitcast_fusion.1
  29.5 0.9 pad_maximum_fusion
  30.5 0.0 all-gather.2.cloned.1.call-update
  30.5 10.3 %all-to-all-start = ((bf16[128,264,128]{2,1,0:T(8,128)(2,1)}), bf16[128,264,128]{2,1,0:T(8,128)(2,1)}, u32[]{:S(2)}, u32[]{:S(2)}) async-start(bf16[128,264,128]{2,1,0:T(8,128)(2,1)} %get-tuple-element.12), calls=%async_computation | async-start | bytes 17301504 | tf_op jit(solution)/shard_map/all_to_all | solution.py:372
  40.8 0.2 reduce-scatter.2.cloned.1.call-start
  41.1 85.6 %all-gather.2.cloned.1.call-done = bf16[24576,128]{1,0:T(8,128)(2,1)} async-done(((bf16[3072,128]{1,0:T(8,128)(2,1)}), bf16[24576,128]{1,0:T(8,128)(2,1)}) %all-gather.2.cloned.1.call-update) | async-done | bytes 6291472 | tf_op jit(solution)/shard_map/all_gather | solution.py:339
  126.6 14.6 %panel.1 = bf16[16,1536,128]{2,1,0:T(8,128)(2,1)} custom-call(s32[1]{0:T(128)} %bitcast.11.x_ref, bf16[1536,768]{1,0:T(8,128)(2,1)} %eta_ref.1, bf16[1536,768]{1,0:T(8,128)(2,1)} %gamma_ref.1, bf16[16,2,768,128]{3,2,1,0:T(8,128)(2,1)} %bitcast.35), custom_call_target="tpu_custom_call" | custom-call | flops 9663676416 | bytes 20971520 | tf_op jit(solution)/shard_map/panel/pallas_call | solution.py:344
  141.2 0.0 copy-start
  141.2 0.0 reduce-scatter.2.cloned.1.call-update
  141.3 0.7 copy-done
  141.9 1.2 copy.27.scale_ref
  143.1 23.2 %all-to-all-done.got_ref = bf16[128,264,128]{2,1,0:T(8,128)(2,1)} async-done(((bf16[128,264,128]{2,1,0:T(8,128)(2,1)}), bf16[128,264,128]{2,1,0:T(8,128)(2,1)}, u32[]{:S(2)}, u32[]{:S(2)}) %all-to-all-start) | async-done | bytes 8650784 | tf_op jit(solution)/shard_map/all_to_all | solution.py:372
  166.3 26.8 %channel.1 = bf16[128,256,128]{2,1,0:T(8,128)(2,1)} custom-call(bf16[128,264,128]{2,1,0:T(8,128)(2,1)} %all-to-all-done.got_ref, bf16[1536,1536]{1,0:T(8,128)(2,1)} %bitcast.36, f32[1536,1]{1,0:T(8,128)} %copy.27.scale_ref), custom_call_target="tpu_custom_call" | custom-call | flops 14495514624 | bytes 23068672 | tf_op jit(solution)/shard_map/channel/pallas_call | solution.py:418
  193.1 111.3 %all_to_all.10.back_ref = bf16[128,256,128]{2,1,0:T(8,128)(2,1)} all-to-all(bf16[128,256,128]{2,1,0:T(8,128)(2,1)} %channel.1), channel_id=1, replica_groups=mesh['row'=8,'col'=16] {'row','col'}, dimensions={0} | all-to-all | bytes 16777216 | tf_op jit(solution)/shard_map/all_to_all | solution.py:372
  304.5 3.4 %reduce-scatter.2.cloned.1.call-done.sums_ref = bf16[1536,128]{1,0:T(8,128)(2,1)} async-done(((bf16[24576,128]{1,0:T(8,128)(2,1)}), bf16[1536,128]{1,0:T(8,128)(2,1)}) %reduce-scatter.2.cloned.1.call-update) | async-done | bytes 393232 | tf_op jit(solution)/shard_map/reduce_scatter | solution.py:366
  307.9 6.8 %update.1 = (bf16[1536,768]{1,0:T(8,128)(2,1)}, bf16[128,1536]{1,0:T(8,128)(2,1)}) custom-call(s32[256]{0:T(256)} %get-tuple-element.9.tile_ref, f32[256]{0:T(256)} %get-tuple-element.10.factor_ref, bf16[128,256,128]{2,1,0:T(8,128)(2,1)} %all_to_all.10.back_ref, bf16[1536,128]{1,0:T(8,128)(2,1)} %reduce-scatter.2.cloned.1.call-done.sums_ref), custom_call_target="tpu_custom_call" | custom-call | bytes 11534336 | tf_op jit(solution)/shard_map/update/pallas_call | solution.py:444
  (1 shorter events, 0.0 us)
Async XLA Ops:
  7.2 11.4 %copy-start.1 = (bf16[1,144]{1,0:T(2,128)(2,1)S(1)}, bf16[1,144]{1,0:T(2,128)(2,1)}, u32[]{:S(2)}) copy-start(bf16[1,144]{1,0:T(2,128)(2,1)} %param.22) | copy-start | bytes 868
  7.2 119.5 %all-gather.2.cloned.1.call-start = ((), (), s32[]{:S(2)}) async-start(), calls=%async_computation.3 | async-start | bytes 7077888 | tf_op jit(solution)/shard_map/all_gather | solution.py:339
  10.0 17.0 %collective-permute-start = (bf16[2,768,128]{2,1,0:T(8,128)(2,1)S(1)}, bf16[2,768,128]{2,1,0:T(8,128)(2,1)S(1)}, u32[]{:S(2)}, u32[]{:S(2)}) collective-permute-start(bf16[2,768,128]{2,1,0:T(8,128)(2,1)S(1)} %fusion.2), channel_id=1, source_target_pairs={{0,65},{1,0},{2,81},{3,16},{4,97},{5,32},{6,113},{7,48},{8,1},{9,6... | collective-permute-start | bytes 1179656 | tf_op jit(solution)/shard_map/ppermute | solution.py:334
  14.1 15.4 %collective-permute-start.1 = (bf16[2,768,128]{2,1,0:T(8,128)(2,1)S(1)}, bf16[2,768,128]{2,1,0:T(8,128)(2,1)S(1)}, u32[]{:S(2)}, u32[]{:S(2)}) collective-permute-start(bf16[2,768,128]{2,1,0:T(8,128)(2,1)S(1)} %fusion), channel_id=1, source_target_pairs={{0,0},{1,65},{2,16},{3,81},{4,32},{5,97},{6,48},{7,113},{8,64},{9,... | collective-permute-start | bytes 1179656 | tf_op jit(solution)/shard_map/ppermute | solution.py:333
  30.5 135.8 %all-to-all-start = ((bf16[128,264,128]{2,1,0:T(8,128)(2,1)}), bf16[128,264,128]{2,1,0:T(8,128)(2,1)}, u32[]{:S(2)}, u32[]{:S(2)}) async-start(bf16[128,264,128]{2,1,0:T(8,128)(2,1)} %get-tuple-element.12), calls=%async_computation | async-start | bytes 17301504 | tf_op jit(solution)/shard_map/all_to_all | solution.py:372
  40.8 267.1 %reduce-scatter.2.cloned.1.call-start = ((), (), s32[]{:S(2)}) async-start(), calls=%async_computation.4 | async-start | bytes 6684672 | tf_op jit(solution)/shard_map/reduce_scatter | solution.py:366
  141.2 0.7 copy-start
Sparse Core Ops, SparseCore 0:
  30.6 95.9 all-gather.1
  141.4 166.4 reduce-scatter.1

commit v6 on v5

--- a/solution.py
+++ b/solution.py
@@ -139,7 +139,7 @@
 
 
 def update_kernel(
-    tile_ref, factor_ref, back_ref, sums_ref, out_ref, turned_ref, held, total, other, sems
+    tile_ref, factor_ref, back_ref, sums_ref, out_ref, turned_ref, held, total, used, sems
 ):
     def copy(j):
         part = pl.ds(j * GROUP, GROUP)
@@ -150,34 +150,47 @@
 
     step_through(BLOCKS // GROUP, 1, begin)
 
+    def note(i, count):
+        for j in range(8):
+            n = i * 8 + j
+            used[count] = n
+            count = count + (factor_ref[n] != 0.0).astype(jnp.int32)
+        return count
+
+    count = lax.fori_loop(0, BLOCKS * CAP // 8, note, 0)
+
     def clear(r):
         total[aligned(r, TILE), :] = jnp.zeros((TILE, COLS), f32)
-        other[aligned(r, TILE), :] = jnp.zeros((TILE, COLS), f32)
 
     step_through(ROWS // TILE, 1, clear)
     turned_ref[...] = sums_ref[...].astype(f32).T.astype(bf16)
 
-    def group(j, carry):
+    def arrive(j, carry):
         copy(j).wait()
-
-        def owner(i):
-            q = j * GROUP + i
-            for k, into in enumerate((total, other)):
-                n = q * CAP + k
-                t = tile_ref[n]
-                rows, cols = aligned(t >> 3, TILE), aligned(t & 7, TILE)
-                into[rows, cols] += factor_ref[n] * held[
-                    q, k * TILE : (k + 1) * TILE, :
-                ].astype(f32)
-
-        step_through(GROUP, 4, owner)
         return carry
 
-    lax.fori_loop(0, BLOCKS // GROUP, group, 0)
+    batch = 8
+
+    def add(i, arrived):
+        last = used[jnp.minimum(i * batch + batch, count) - 1]
+        needed = last // (GROUP * CAP) + 1
+        lax.fori_loop(arrived, needed, arrive, 0)
+        for j in range(batch):
+            e = i * batch + j
+            n = jnp.where(e < count, used[e], 0)
+            factor = jnp.where(e < count, factor_ref[n], 0.0)
+            t = tile_ref[n]
+            rows, cols = aligned(t >> 3, TILE), aligned(t & 7, TILE)
+            at = pl.ds(pl.multiple_of((n & 1) * TILE, TILE), TILE)
+            total[rows, cols] += factor * held[n >> 1, at, :].astype(f32)
+        return jnp.maximum(arrived, needed)
+
+    arrived = lax.fori_loop(0, (count + batch - 1) // batch, add, 0)
+    lax.fori_loop(arrived, BLOCKS // GROUP, arrive, 0)
 
     def finish(r):
         rows = aligned(r, TILE)
-        out_ref[rows, :] = (total[rows, :] + other[rows, :]).astype(bf16)
+        out_ref[rows, :] = total[rows, :].astype(bf16)
 
     step_through(ROWS // TILE, 1, finish)
 
@@ -260,9 +273,11 @@
         scale = scale_ref[...]
         gamma_scaled = (scale * gamma_ref[:, cols].astype(f32)).astype(bf16)
         eta_scaled = (-scale * eta[:, cols].astype(f32)).astype(bf16)
-        part = jnp.dot(eta[...], gamma_scaled, preferred_element_type=f32)
-        part += jnp.dot(gamma_ref[...], eta_scaled, preferred_element_type=f32)
-        product[:, cols] = part.astype(bf16)
+        for h in range(2):
+            rows = pl.ds(h * width, width)
+            part = jnp.dot(eta[rows, :], gamma_scaled, preferred_element_type=f32)
+            part += jnp.dot(gamma_ref[rows, :], eta_scaled, preferred_element_type=f32)
+            product[rows, cols] = part.astype(bf16)
 
     step_through(PH_STATES // width, 1, multiply)
 
@@ -449,7 +464,12 @@
             jax.ShapeDtypeStruct((ROWS, COLS), bf16),
             jax.ShapeDtypeStruct((PANEL_DEV, ROWS), bf16),
         ],
-        scratch_shapes=[held] + [pltpu.VMEM((ROWS, COLS), f32)] * 2 + [dma((groups,))],
+        scratch_shapes=[
+            held,
+            pltpu.VMEM((ROWS, COLS), f32),
+            pltpu.SMEM((slots + 8,), jnp.int32),
+            dma((groups,)),
+        ],
         compiler_params=params(),
         cost_estimate=pl.CostEstimate(flops=0, bytes_accessed=11 << 20, transcendentals=0),
         name="update",

time: 324 us -> 323 us (level)
  no operation moved by 1% of the time
where the time goes in v6:
time: 323 us; the launch traced here: 321 us
  blocking collectives  114 us (35%)
  waiting for transfers between devices  112 us (35%)
  Pallas kernels  54.9 us (17%)
  starting transfers between devices  18.2 us (6%)
  between operations  14.9 us (5%)
  other arithmetic  4.34 us (1%)
    all_to_all x1, blocking collectives, exchange(): lax.all_to_all(tiles, ('row', 'col'), split_axis=0, concat_axis=0, tiled=...  114 us
    all_gather x1, waiting for transfers between devices, panel_part(): lax.all_gather(pieces.reshape(4 * COLS, PANEL_DEV), 'row', axis=0, tiled=...  85.8 us
    pallas_call x1, Pallas kernels, updates(): pl.pallas_call(channel_kernel, in_specs=[any_spec(), any_spec(), vmem_spe...  26.5 us
    all_to_all x1, waiting for transfers between devices, exchange(): lax.all_to_all(tiles, ('row', 'col'), split_axis=0, concat_axis=0, tiled=...  23.2 us
    pallas_call x1, Pallas kernels, panel_part(): pl.pallas_call(panel_kernel, grid_spec=pltpu.PrefetchScalarGridSpec(num_s...  14.6 us
    all_to_all x1, starting transfers between devices, exchange(): lax.all_to_all(tiles, ('row', 'col'), split_axis=0, concat_axis=0, tiled=...  10.3 us
    pallas_call x1, Pallas kernels, updates(): pl.pallas_call(send_kernel, in_specs=[smem_spec()] * 5 + [any_spec()], ou...  7.25 us
    pallas_call x1, Pallas kernels, updates(): pl.pallas_call(update_kernel, in_specs=[smem_spec(), smem_spec(), any_spe...  6.56 us
  transfers between devices with their start and end apart: 5, of which 4 were waited for; matrix products, arithmetic and copies ran while one was open for 1% of the time, Pallas kernels for 13%

profile of v6, /device:TPU:8, one launch (start us, length us, event | category | flops | bytes accessed | tf_op | source)
XLA Modules:
  0.0 320.6 jit_solution(8090005736638221287)
XLA Ops:
  7.2 0.0 copy-start.1
  7.2 0.0 all-gather.2.cloned.1.call-start
  7.2 1.2 select_reduce_fusion.1
  8.5 1.4 multiply_convert_fusion.1
  9.9 0.1 fusion.2
  10.0 4.1 %collective-permute-start = (bf16[2,768,128]{2,1,0:T(8,128)(2,1)S(1)}, bf16[2,768,128]{2,1,0:T(8,128)(2,1)S(1)}, u32[]{:S(2)}, u32[]{:S(2)}) collective-permute-start(bf16[2,768,128]{2,1,0:T(8,128)(2,1)S(1)} %fusion.2), channel_id=1, source_target_pairs={{0,65},{1,0},{2,81},{3,16},{4,97},{5,32},{6,113},{7,48},{8,1},{9,6... | collective-permute-start | bytes 1179656 | tf_op jit(solution)/shard_map/ppermute | solution.py:349
  14.0 0.1 fusion
  14.1 3.8 %collective-permute-start.1 = (bf16[2,768,128]{2,1,0:T(8,128)(2,1)S(1)}, bf16[2,768,128]{2,1,0:T(8,128)(2,1)S(1)}, u32[]{:S(2)}, u32[]{:S(2)}) collective-permute-start(bf16[2,768,128]{2,1,0:T(8,128)(2,1)S(1)} %fusion), channel_id=1, source_target_pairs={{0,0},{1,65},{2,16},{3,81},{4,32},{5,97},{6,48},{7,113},{8,64},{9,... | collective-permute-start | bytes 1179656 | tf_op jit(solution)/shard_map/ppermute | solution.py:348
  18.5 0.0 copy-done.1
  18.6 0.6 convert_element_type.15.weight_ref
  19.1 7.2 %send.1 = (bf16[128,264,128]{2,1,0:T(8,128)(2,1)}, s32[256]{0:T(256)}, f32[256]{0:T(256)}) custom-call(s32[1]{0:T(128)S(6)} %copy.29.live_ref, s32[1,144]{1,0:T(1,128)} %source_ref.1, s32[1,144]{1,0:T(1,128)} %owner_ref.1, s32[1,144]{1,0:T(1,128)} %place_ref.1, f32[1,144]{1,0:T(1,128)} %convert_element_type.15.weight_ref, bf16[1536,768]{1,0:T(8,128)(2,1)} %eta_ref.1), custom_call_target="tpu_custom_call" | custom-call | bytes 11534336 | tf_op jit(solution)/shard_map/send/pallas_call | solution.py:408
  26.4 0.0 collective-permute-done
  26.4 3.1 collective-permute-done.1
  29.5 0.1 select_bitcast_fusion.1
  29.5 0.9 pad_maximum_fusion
  30.5 0.0 all-gather.2.cloned.1.call-update
  30.5 10.3 %all-to-all-start = ((bf16[128,264,128]{2,1,0:T(8,128)(2,1)}), bf16[128,264,128]{2,1,0:T(8,128)(2,1)}, u32[]{:S(2)}, u32[]{:S(2)}) async-start(bf16[128,264,128]{2,1,0:T(8,128)(2,1)} %get-tuple-element.12), calls=%async_computation | async-start | bytes 17301504 | tf_op jit(solution)/shard_map/all_to_all | solution.py:387
  40.8 0.0 reduce-scatter.2.cloned.1.call-start
  40.9 85.8 %all-gather.2.cloned.1.call-done = bf16[24576,128]{1,0:T(8,128)(2,1)} async-done(((bf16[3072,128]{1,0:T(8,128)(2,1)}), bf16[24576,128]{1,0:T(8,128)(2,1)}) %all-gather.2.cloned.1.call-update) | async-done | bytes 6291472 | tf_op jit(solution)/shard_map/all_gather | solution.py:354
  126.6 14.6 %panel.1 = bf16[16,1536,128]{2,1,0:T(8,128)(2,1)} custom-call(s32[1]{0:T(128)} %bitcast.11.x_ref, bf16[1536,768]{1,0:T(8,128)(2,1)} %eta_ref.1, bf16[1536,768]{1,0:T(8,128)(2,1)} %gamma_ref.1, bf16[16,2,768,128]{3,2,1,0:T(8,128)(2,1)} %bitcast.35), custom_call_target="tpu_custom_call" | custom-call | flops 9663676416 | bytes 20971520 | tf_op jit(solution)/shard_map/panel/pallas_call | solution.py:359
  141.2 0.0 copy-start
  141.2 0.0 reduce-scatter.2.cloned.1.call-update
  141.3 0.7 copy-done
  141.9 1.2 copy.27.scale_ref
  143.1 23.2 %all-to-all-done.got_ref = bf16[128,264,128]{2,1,0:T(8,128)(2,1)} async-done(((bf16[128,264,128]{2,1,0:T(8,128)(2,1)}), bf16[128,264,128]{2,1,0:T(8,128)(2,1)}, u32[]{:S(2)}, u32[]{:S(2)}) %all-to-all-start) | async-done | bytes 8650784 | tf_op jit(solution)/shard_map/all_to_all | solution.py:387
  166.3 26.5 %channel.1 = bf16[128,256,128]{2,1,0:T(8,128)(2,1)} custom-call(bf16[128,264,128]{2,1,0:T(8,128)(2,1)} %all-to-all-done.got_ref, bf16[1536,1536]{1,0:T(8,128)(2,1)} %bitcast.36, f32[1536,1]{1,0:T(8,128)} %copy.27.scale_ref), custom_call_target="tpu_custom_call" | custom-call | flops 14495514624 | bytes 23068672 | tf_op jit(solution)/shard_map/channel/pallas_call | solution.py:433
  192.8 114.0 %all_to_all.10.back_ref = bf16[128,256,128]{2,1,0:T(8,128)(2,1)} all-to-all(bf16[128,256,128]{2,1,0:T(8,128)(2,1)} %channel.1), channel_id=1, replica_groups=mesh['row'=8,'col'=16] {'row','col'}, dimensions={0} | all-to-all | bytes 16777216 | tf_op jit(solution)/shard_map/all_to_all | solution.py:387
  306.8 0.4 reduce-scatter.2.cloned.1.call-done.sums_ref
  307.2 6.6 %update.1 = (bf16[1536,768]{1,0:T(8,128)(2,1)}, bf16[128,1536]{1,0:T(8,128)(2,1)}) custom-call(s32[256]{0:T(256)} %get-tuple-element.9.tile_ref, f32[256]{0:T(256)} %get-tuple-element.10.factor_ref, bf16[128,256,128]{2,1,0:T(8,128)(2,1)} %all_to_all.10.back_ref, bf16[1536,128]{1,0:T(8,128)(2,1)} %reduce-scatter.2.cloned.1.call-done.sums_ref), custom_call_target="tpu_custom_call" | custom-call | bytes 11534336 | tf_op jit(solution)/shard_map/update/pallas_call | solution.py:459
  (1 shorter events, 0.0 us)
Async XLA Ops:
  7.2 11.4 %copy-start.1 = (bf16[1,144]{1,0:T(2,128)(2,1)S(1)}, bf16[1,144]{1,0:T(2,128)(2,1)}, u32[]{:S(2)}) copy-start(bf16[1,144]{1,0:T(2,128)(2,1)} %param.22) | copy-start | bytes 868
  7.2 119.5 %all-gather.2.cloned.1.call-start = ((), (), s32[]{:S(2)}) async-start(), calls=%async_computation.3 | async-start | bytes 7077888 | tf_op jit(solution)/shard_map/all_gather | solution.py:354
  10.0 16.4 %collective-permute-start = (bf16[2,768,128]{2,1,0:T(8,128)(2,1)S(1)}, bf16[2,768,128]{2,1,0:T(8,128)(2,1)S(1)}, u32[]{:S(2)}, u32[]{:S(2)}) collective-permute-start(bf16[2,768,128]{2,1,0:T(8,128)(2,1)S(1)} %fusion.2), channel_id=1, source_target_pairs={{0,65},{1,0},{2,81},{3,16},{4,97},{5,32},{6,113},{7,48},{8,1},{9,6... | collective-permute-start | bytes 1179656 | tf_op jit(solution)/shard_map/ppermute | solution.py:349
  14.1 15.4 %collective-permute-start.1 = (bf16[2,768,128]{2,1,0:T(8,128)(2,1)S(1)}, bf16[2,768,128]{2,1,0:T(8,128)(2,1)S(1)}, u32[]{:S(2)}, u32[]{:S(2)}) collective-permute-start(bf16[2,768,128]{2,1,0:T(8,128)(2,1)S(1)} %fusion), channel_id=1, source_target_pairs={{0,0},{1,65},{2,16},{3,81},{4,32},{5,97},{6,48},{7,113},{8,64},{9,... | collective-permute-start | bytes 1179656 | tf_op jit(solution)/shard_map/ppermute | solution.py:348
  30.5 135.8 %all-to-all-start = ((bf16[128,264,128]{2,1,0:T(8,128)(2,1)}), bf16[128,264,128]{2,1,0:T(8,128)(2,1)}, u32[]{:S(2)}, u32[]{:S(2)}) async-start(bf16[128,264,128]{2,1,0:T(8,128)(2,1)} %get-tuple-element.12), calls=%async_computation | async-start | bytes 17301504 | tf_op jit(solution)/shard_map/all_to_all | solution.py:387
  40.8 266.4 %reduce-scatter.2.cloned.1.call-start = ((), (), s32[]{:S(2)}) async-start(), calls=%async_computation.4 | async-start | bytes 6684672 | tf_op jit(solution)/shard_map/reduce_scatter | solution.py:381
  141.2 0.7 copy-start
Sparse Core Ops, SparseCore 0:
  30.6 95.9 all-gather.1
  141.4 165.8 reduce-scatter.1

commit v7 on v6

--- a/solution.py
+++ b/solution.py
@@ -92,7 +92,8 @@
     step_through(BLOCKS, 8, clear_count)
 
     def slot(s, carry):
-        q = owner_ref[0, s]
+        owner = owner_ref[0, s]
+        q = (owner & (N_COL - 1)) * N_ROW + owner // N_COL
         k = counts[q]
         counts[q] = k + 1
         n = q * CAP + k
@@ -138,8 +139,12 @@
     step_through(BLOCKS // GROUP, 1, finish)
 
 
+def turn_kernel(in_ref, out_ref):
+    out_ref[...] = in_ref[...].astype(f32).T.astype(bf16)
+
+
 def update_kernel(
-    tile_ref, factor_ref, back_ref, sums_ref, out_ref, turned_ref, held, total, used, sems
+    tile_ref, factor_ref, back_ref, out_ref, held, total, used, sems
 ):
     def copy(j):
         part = pl.ds(j * GROUP, GROUP)
@@ -163,7 +168,6 @@
         total[aligned(r, TILE), :] = jnp.zeros((TILE, COLS), f32)
 
     step_through(ROWS // TILE, 1, clear)
-    turned_ref[...] = sums_ref[...].astype(f32).T.astype(bf16)
 
     def arrive(j, carry):
         copy(j).wait()
@@ -384,7 +388,7 @@
 
 
 def exchange(tiles):
-    return lax.all_to_all(tiles, ("row", "col"), split_axis=0, concat_axis=0, tiled=True)
+    return lax.all_to_all(tiles, ("col", "row"), split_axis=0, concat_axis=0, tiled=True)
 
 
 def updates(
@@ -456,14 +460,11 @@
         name="channel",
     )(received, gamma_recoupled[0], ph_factor.reshape(PH_STATES, 1))
     returned = exchange(answers)
-    recoupled_update, panel_update = pl.pallas_call(
+    recoupled_update = pl.pallas_call(
         update_kernel,
-        in_specs=[smem_spec(), smem_spec(), any_spec(), vmem_spec()],
-        out_specs=[vmem_spec(), vmem_spec()],
-        out_shape=[
-            jax.ShapeDtypeStruct((ROWS, COLS), bf16),
-            jax.ShapeDtypeStruct((PANEL_DEV, ROWS), bf16),
-        ],
+        in_specs=[smem_spec(), smem_spec(), any_spec()],
+        out_specs=vmem_spec(),
+        out_shape=jax.ShapeDtypeStruct((ROWS, COLS), bf16),
         scratch_shapes=[
             held,
             pltpu.VMEM((ROWS, COLS), f32),
@@ -473,7 +474,15 @@
         compiler_params=params(),
         cost_estimate=pl.CostEstimate(flops=0, bytes_accessed=11 << 20, transcendentals=0),
         name="update",
-    )(tiles, factors, returned, panel_sums)
+    )(tiles, factors, returned)
+    panel_update = pl.pallas_call(
+        turn_kernel,
+        in_specs=[vmem_spec()],
+        out_specs=vmem_spec(),
+        out_shape=jax.ShapeDtypeStruct((PANEL_DEV, ROWS), bf16),
+        compiler_params=params(),
+        name="turn",
+    )(panel_sums)
     return (panel_update, recoupled_update)
 
 

time: 323 us -> 319 us (0.988)
  blocking collectives: 114 us -> 105 us
    all_to_all x1, blocking collectives: 114 us -> 105 us  [exchange(): lax.all_to_all(tiles, ('col', 'row'), split_axis=0, concat_axis=0, tiled=...]
  transfers between devices with their start and end apart: 5 -> 5, of which waited for: 4 -> 4; matrix products, arithmetic and copies ran while one was open for 1% -> 1% of each run, Pallas kernels for 13% -> 15%
where the time goes in v7:
time: 319 us; the launch traced here: 315 us
  waiting for transfers between devices  114 us (36%)
  blocking collectives  105 us (33%)
  Pallas kernels  57.2 us (18%)
  starting transfers between devices  18.2 us (6%)
  between operations  14.8 us (5%)
  other arithmetic  4.34 us (1%)
    all_to_all x1, blocking collectives, exchange(): lax.all_to_all(tiles, ('col', 'row'), split_axis=0, concat_axis=0, tiled=...  105 us
    all_gather x1, waiting for transfers between devices, panel_part(): lax.all_gather(pieces.reshape(4 * COLS, PANEL_DEV), 'row', axis=0, tiled=...  83.2 us
    pallas_call x1, Pallas kernels, updates(): pl.pallas_call(channel_kernel, in_specs=[any_spec(), any_spec(), vmem_spe...  26.6 us
    all_to_all x1, waiting for transfers between devices, exchange(): lax.all_to_all(tiles, ('col', 'row'), split_axis=0, concat_axis=0, tiled=...  26.2 us
    pallas_call x1, Pallas kernels, panel_part(): pl.pallas_call(panel_kernel, grid_spec=pltpu.PrefetchScalarGridSpec(num_s...  14.6 us
    all_to_all x1, starting transfers between devices, exchange(): lax.all_to_all(tiles, ('col', 'row'), split_axis=0, concat_axis=0, tiled=...  10.3 us
    pallas_call x1, Pallas kernels, updates(): pl.pallas_call(send_kernel, in_specs=[smem_spec()] * 5 + [any_spec()], ou...  7.98 us
  transfers between devices with their start and end apart: 5, of which 4 were waited for; matrix products, arithmetic and copies ran while one was open for 1% of the time, Pallas kernels for 15%

profile of v7, /device:TPU:8, one launch (start us, length us, event | category | flops | bytes accessed | tf_op | source)
XLA Modules:
  0.0 315.4 jit_solution(16692666540736762112)
XLA Ops:
  7.2 0.0 copy-start.1
  7.2 0.0 all-gather.2.cloned.1.call-start
  7.2 1.2 select_reduce_fusion.1
  8.5 1.4 multiply_convert_fusion.1
  9.9 0.1 fusion.2
  10.0 4.1 %collective-permute-start = (bf16[2,768,128]{2,1,0:T(8,128)(2,1)S(1)}, bf16[2,768,128]{2,1,0:T(8,128)(2,1)S(1)}, u32[]{:S(2)}, u32[]{:S(2)}) collective-permute-start(bf16[2,768,128]{2,1,0:T(8,128)(2,1)S(1)} %fusion.2), channel_id=1, source_target_pairs={{0,65},{1,0},{2,81},{3,16},{4,97},{5,32},{6,113},{7,48},{8,1},{9,6... | collective-permute-start | bytes 1179656 | tf_op jit(solution)/shard_map/ppermute | solution.py:353
  14.0 0.1 fusion
  14.1 3.8 %collective-permute-start.1 = (bf16[2,768,128]{2,1,0:T(8,128)(2,1)S(1)}, bf16[2,768,128]{2,1,0:T(8,128)(2,1)S(1)}, u32[]{:S(2)}, u32[]{:S(2)}) collective-permute-start(bf16[2,768,128]{2,1,0:T(8,128)(2,1)S(1)} %fusion), channel_id=1, source_target_pairs={{0,0},{1,65},{2,16},{3,81},{4,32},{5,97},{6,48},{7,113},{8,64},{9,... | collective-permute-start | bytes 1179656 | tf_op jit(solution)/shard_map/ppermute | solution.py:352
  17.9 0.0 copy-done.1
  17.9 0.6 convert_element_type.15.weight_ref
  19.1 8.0 %send.1 = (bf16[128,264,128]{2,1,0:T(8,128)(2,1)}, s32[256]{0:T(256)}, f32[256]{0:T(256)}) custom-call(s32[1]{0:T(128)S(6)} %copy.29.live_ref, s32[1,144]{1,0:T(1,128)} %source_ref.1, s32[1,144]{1,0:T(1,128)} %owner_ref.1, s32[1,144]{1,0:T(1,128)} %place_ref.1, f32[1,144]{1,0:T(1,128)} %convert_element_type.15.weight_ref, bf16[1536,768]{1,0:T(8,128)(2,1)} %eta_ref.1), custom_call_target="tpu_custom_call" | custom-call | bytes 11534336 | tf_op jit(solution)/shard_map/send/pallas_call | solution.py:412
  27.1 0.0 collective-permute-done
  27.1 2.3 collective-permute-done.1
  29.5 0.1 select_bitcast_fusion.1
  29.5 0.9 pad_maximum_fusion
  30.5 0.0 all-gather.2.cloned.1.call-update
  30.5 10.3 %all-to-all-start = ((bf16[128,264,128]{2,1,0:T(8,128)(2,1)}), bf16[128,264,128]{2,1,0:T(8,128)(2,1)}, u32[]{:S(2)}, u32[]{:S(2)}) async-start(bf16[128,264,128]{2,1,0:T(8,128)(2,1)} %get-tuple-element.11), calls=%async_computation.1 | async-start | bytes 17301504 | tf_op jit(solution)/shard_map/all_to_all | solution.py:391
  40.8 0.0 reduce-scatter.2.cloned.1.call-start
  40.9 83.2 %all-gather.2.cloned.1.call-done = bf16[24576,128]{1,0:T(8,128)(2,1)} async-done(((bf16[3072,128]{1,0:T(8,128)(2,1)}), bf16[24576,128]{1,0:T(8,128)(2,1)}) %all-gather.2.cloned.1.call-update) | async-done | bytes 6291472 | tf_op jit(solution)/shard_map/all_gather | solution.py:358
  124.1 14.6 %panel.1 = bf16[16,1536,128]{2,1,0:T(8,128)(2,1)} custom-call(s32[1]{0:T(128)} %bitcast.x_ref, bf16[1536,768]{1,0:T(8,128)(2,1)} %eta_ref.1, bf16[1536,768]{1,0:T(8,128)(2,1)} %gamma_ref.1, bf16[16,2,768,128]{3,2,1,0:T(8,128)(2,1)} %bitcast.35), custom_call_target="tpu_custom_call" | custom-call | flops 9663676416 | bytes 20971520 | tf_op jit(solution)/shard_map/panel/pallas_call | solution.py:363
  138.6 0.0 copy-start
  138.6 0.0 reduce-scatter.2.cloned.1.call-update
  138.7 0.7 copy-done
  139.3 1.2 copy.27.scale_ref
  140.5 26.2 %all-to-all-done.got_ref = bf16[128,264,128]{2,1,0:T(8,128)(2,1)} async-done(((bf16[128,264,128]{2,1,0:T(8,128)(2,1)}), bf16[128,264,128]{2,1,0:T(8,128)(2,1)}, u32[]{:S(2)}, u32[]{:S(2)}) %all-to-all-start) | async-done | bytes 8650784 | tf_op jit(solution)/shard_map/all_to_all | solution.py:391
  166.7 26.6 %channel.1 = bf16[128,256,128]{2,1,0:T(8,128)(2,1)} custom-call(bf16[128,264,128]{2,1,0:T(8,128)(2,1)} %all-to-all-done.got_ref, bf16[1536,1536]{1,0:T(8,128)(2,1)} %bitcast.36, f32[1536,1]{1,0:T(8,128)} %copy.27.scale_ref), custom_call_target="tpu_custom_call" | custom-call | flops 14495514624 | bytes 23068672 | tf_op jit(solution)/shard_map/channel/pallas_call | solution.py:437
  193.3 104.6 %all_to_all.10.back_ref = bf16[128,256,128]{2,1,0:T(8,128)(2,1)} all-to-all(bf16[128,256,128]{2,1,0:T(8,128)(2,1)} %channel.1), channel_id=1, replica_groups=mesh['row'=8,'col'=16] {'col','row'}, dimensions={0} | all-to-all | bytes 16777216 | tf_op jit(solution)/shard_map/all_to_all | solution.py:391
  297.9 6.1 %update.1 = bf16[1536,768]{1,0:T(8,128)(2,1)} custom-call(s32[256]{0:T(256)} %get-tuple-element.9.tile_ref, f32[256]{0:T(256)} %get-tuple-element.10.factor_ref, bf16[128,256,128]{2,1,0:T(8,128)(2,1)} %all_to_all.10.back_ref), custom_call_target="tpu_custom_call" | custom-call | bytes 11534336 | tf_op jit(solution)/shard_map/update/pallas_call | solution.py:463
  304.0 2.6 reduce-scatter.2.cloned.1.call-done.in_ref
  306.6 1.9 turn.1
  (1 shorter events, 0.0 us)
Async XLA Ops:
  7.2 10.7 %copy-start.1 = (bf16[1,144]{1,0:T(2,128)(2,1)S(1)}, bf16[1,144]{1,0:T(2,128)(2,1)}, u32[]{:S(2)}) copy-start(bf16[1,144]{1,0:T(2,128)(2,1)} %param.22) | copy-start | bytes 868
  7.2 116.9 %all-gather.2.cloned.1.call-start = ((), (), s32[]{:S(2)}) async-start(), calls=%async_computation.3 | async-start | bytes 7077888 | tf_op jit(solution)/shard_map/all_gather | solution.py:358
  10.0 17.1 %collective-permute-start = (bf16[2,768,128]{2,1,0:T(8,128)(2,1)S(1)}, bf16[2,768,128]{2,1,0:T(8,128)(2,1)S(1)}, u32[]{:S(2)}, u32[]{:S(2)}) collective-permute-start(bf16[2,768,128]{2,1,0:T(8,128)(2,1)S(1)} %fusion.2), channel_id=1, source_target_pairs={{0,65},{1,0},{2,81},{3,16},{4,97},{5,32},{6,113},{7,48},{8,1},{9,6... | collective-permute-start | bytes 1179656 | tf_op jit(solution)/shard_map/ppermute | solution.py:353
  14.1 15.4 %collective-permute-start.1 = (bf16[2,768,128]{2,1,0:T(8,128)(2,1)S(1)}, bf16[2,768,128]{2,1,0:T(8,128)(2,1)S(1)}, u32[]{:S(2)}, u32[]{:S(2)}) collective-permute-start(bf16[2,768,128]{2,1,0:T(8,128)(2,1)S(1)} %fusion), channel_id=1, source_target_pairs={{0,0},{1,65},{2,16},{3,81},{4,32},{5,97},{6,48},{7,113},{8,64},{9,... | collective-permute-start | bytes 1179656 | tf_op jit(solution)/shard_map/ppermute | solution.py:352
  30.5 136.2 %all-to-all-start = ((bf16[128,264,128]{2,1,0:T(8,128)(2,1)}), bf16[128,264,128]{2,1,0:T(8,128)(2,1)}, u32[]{:S(2)}, u32[]{:S(2)}) async-start(bf16[128,264,128]{2,1,0:T(8,128)(2,1)} %get-tuple-element.11), calls=%async_computation.1 | async-start | bytes 17301504 | tf_op jit(solution)/shard_map/all_to_all | solution.py:391
  40.8 265.8 %reduce-scatter.2.cloned.1.call-start = ((), (), s32[]{:S(2)}) async-start(), calls=%async_computation.4 | async-start | bytes 6684672 | tf_op jit(solution)/shard_map/reduce_scatter | solution.py:385
  138.6 0.7 copy-start
Sparse Core Ops, SparseCore 0:
  30.6 93.3 all-gather.1
  138.8 167.7 reduce-scatter.1

commit v8 on v7

--- a/solution.py
+++ b/solution.py
@@ -364,16 +364,16 @@
         panel_kernel,
         grid_spec=pltpu.PrefetchScalarGridSpec(
             num_scalar_prefetch=1,
-            grid=(SIDE,),
+            grid=(2, SIDE),
             in_specs=[
-                pl.BlockSpec((ROWS, COLS), lambda y, x: (0, 0)),
-                pl.BlockSpec((ROWS, COLS), lambda y, x: (0, 0)),
+                pl.BlockSpec((ROWS // 2, COLS), lambda r, y, x: (r, 0)),
+                pl.BlockSpec((ROWS // 2, COLS), lambda r, y, x: (r, 0)),
                 pl.BlockSpec(
                     (SIDE, 2, COLS, PANEL_DEV),
-                    lambda y, x: (lax.rem(y + x[0], SIDE), 0, 0, 0),
+                    lambda r, y, x: (lax.rem(y + x[0], SIDE), 0, 0, 0),
                 ),
             ],
-            out_specs=pl.BlockSpec((SIDE, ROWS, PANEL_DEV), lambda y, x: (y, 0, 0)),
+            out_specs=pl.BlockSpec((SIDE, ROWS // 2, PANEL_DEV), lambda r, y, x: (y, r, 0)),
         ),
         out_shape=jax.ShapeDtypeStruct((N_COL, ROWS, PANEL_DEV), bf16),
         compiler_params=params(),

time: 319 us -> 319 us (level)
  no operation moved by 1% of the time
where the time goes in v8:
time: 319 us; the launch traced here: 316 us
  waiting for transfers between devices  113 us (35%)
  blocking collectives  105 us (33%)
  Pallas kernels  59.1 us (19%)
  starting transfers between devices  18.9 us (6%)
  between operations  14.8 us (5%)
  other arithmetic  4.34 us (1%)
    all_to_all x1, blocking collectives, exchange(): lax.all_to_all(tiles, ('col', 'row'), split_axis=0, concat_axis=0, tiled=...  105 us
    all_gather x1, waiting for transfers between devices, panel_part(): lax.all_gather(pieces.reshape(4 * COLS, PANEL_DEV), 'row', axis=0, tiled=...  83.2 us
    pallas_call x1, Pallas kernels, updates(): pl.pallas_call(channel_kernel, in_specs=[any_spec(), any_spec(), vmem_spe...  26.6 us
    all_to_all x1, waiting for transfers between devices, exchange(): lax.all_to_all(tiles, ('col', 'row'), split_axis=0, concat_axis=0, tiled=...  24.8 us
    pallas_call x1, Pallas kernels, panel_part(): pl.pallas_call(panel_kernel, grid_spec=pltpu.PrefetchScalarGridSpec(num_s...  15.9 us
    all_to_all x1, starting transfers between devices, exchange(): lax.all_to_all(tiles, ('col', 'row'), split_axis=0, concat_axis=0, tiled=...  11 us
    pallas_call x1, Pallas kernels, updates(): pl.pallas_call(send_kernel, in_specs=[smem_spec()] * 5 + [any_spec()], ou...  8.48 us
  transfers between devices with their start and end apart: 5, of which 4 were waited for; matrix products, arithmetic and copies ran while one was open for 1% of the time, Pallas kernels for 15%

profile of v8, /device:TPU:8, one launch (start us, length us, event | category | flops | bytes accessed | tf_op | source)
XLA Modules:
  0.0 316.2 jit_solution(10424389381151005796)
XLA Ops:
  7.2 0.0 copy-start.1
  7.2 0.0 all-gather.2.cloned.1.call-start
  7.2 1.2 select_reduce_fusion.1
  8.5 1.4 multiply_convert_fusion.1
  9.9 0.1 fusion.2
  10.0 4.1 %collective-permute-start = (bf16[2,768,128]{2,1,0:T(8,128)(2,1)S(1)}, bf16[2,768,128]{2,1,0:T(8,128)(2,1)S(1)}, u32[]{:S(2)}, u32[]{:S(2)}) collective-permute-start(bf16[2,768,128]{2,1,0:T(8,128)(2,1)S(1)} %fusion.2), channel_id=1, source_target_pairs={{0,65},{1,0},{2,81},{3,16},{4,97},{5,32},{6,113},{7,48},{8,1},{9,6... | collective-permute-start | bytes 1179656 | tf_op jit(solution)/shard_map/ppermute | solution.py:353
  14.0 0.1 fusion
  14.1 3.8 %collective-permute-start.1 = (bf16[2,768,128]{2,1,0:T(8,128)(2,1)S(1)}, bf16[2,768,128]{2,1,0:T(8,128)(2,1)S(1)}, u32[]{:S(2)}, u32[]{:S(2)}) collective-permute-start(bf16[2,768,128]{2,1,0:T(8,128)(2,1)S(1)} %fusion), channel_id=1, source_target_pairs={{0,0},{1,65},{2,16},{3,81},{4,32},{5,97},{6,48},{7,113},{8,64},{9,... | collective-permute-start | bytes 1179656 | tf_op jit(solution)/shard_map/ppermute | solution.py:352
  17.9 0.0 copy-done.1
  17.9 0.6 convert_element_type.15.weight_ref
  19.1 8.5 %send.1 = (bf16[128,264,128]{2,1,0:T(8,128)(2,1)}, s32[256]{0:T(256)}, f32[256]{0:T(256)}) custom-call(s32[1]{0:T(128)S(6)} %copy.29.live_ref, s32[1,144]{1,0:T(1,128)} %source_ref.1, s32[1,144]{1,0:T(1,128)} %owner_ref.1, s32[1,144]{1,0:T(1,128)} %place_ref.1, f32[1,144]{1,0:T(1,128)} %convert_element_type.15.weight_ref, bf16[1536,768]{1,0:T(8,128)(2,1)} %eta_ref.1), custom_call_target="tpu_custom_call" | custom-call | bytes 11534336 | tf_op jit(solution)/shard_map/send/pallas_call | solution.py:412
  27.6 0.0 collective-permute-done
  27.6 1.8 collective-permute-done.1
  29.5 0.1 select_bitcast_fusion.1
  29.5 0.9 pad_maximum_fusion
  30.5 0.0 all-gather.2.cloned.1.call-update
  30.5 11.0 %all-to-all-start = ((bf16[128,264,128]{2,1,0:T(8,128)(2,1)}), bf16[128,264,128]{2,1,0:T(8,128)(2,1)}, u32[]{:S(2)}, u32[]{:S(2)}) async-start(bf16[128,264,128]{2,1,0:T(8,128)(2,1)} %get-tuple-element.11), calls=%async_computation.1 | async-start | bytes 17301504 | tf_op jit(solution)/shard_map/all_to_all | solution.py:391
  41.5 0.0 reduce-scatter.2.cloned.1.call-start
  41.6 83.2 %all-gather.2.cloned.1.call-done = bf16[24576,128]{1,0:T(8,128)(2,1)} async-done(((bf16[3072,128]{1,0:T(8,128)(2,1)}), bf16[24576,128]{1,0:T(8,128)(2,1)}) %all-gather.2.cloned.1.call-update) | async-done | bytes 6291472 | tf_op jit(solution)/shard_map/all_gather | solution.py:358
  124.7 15.9 %panel.1 = bf16[16,1536,128]{2,1,0:T(8,128)(2,1)} custom-call(s32[1]{0:T(128)} %bitcast.x_ref, bf16[1536,768]{1,0:T(8,128)(2,1)} %eta_ref.1, bf16[1536,768]{1,0:T(8,128)(2,1)} %gamma_ref.1, bf16[16,2,768,128]{3,2,1,0:T(8,128)(2,1)} %bitcast.35), custom_call_target="tpu_custom_call" | custom-call | flops 9663676416 | bytes 20971520 | tf_op jit(solution)/shard_map/panel/pallas_call | solution.py:363
  140.7 0.0 copy-start
  140.7 0.0 reduce-scatter.2.cloned.1.call-update
  140.7 0.7 copy-done
  141.4 1.2 copy.27.scale_ref
  142.6 24.8 %all-to-all-done.got_ref = bf16[128,264,128]{2,1,0:T(8,128)(2,1)} async-done(((bf16[128,264,128]{2,1,0:T(8,128)(2,1)}), bf16[128,264,128]{2,1,0:T(8,128)(2,1)}, u32[]{:S(2)}, u32[]{:S(2)}) %all-to-all-start) | async-done | bytes 8650784 | tf_op jit(solution)/shard_map/all_to_all | solution.py:391
  167.4 26.6 %channel.1 = bf16[128,256,128]{2,1,0:T(8,128)(2,1)} custom-call(bf16[128,264,128]{2,1,0:T(8,128)(2,1)} %all-to-all-done.got_ref, bf16[1536,1536]{1,0:T(8,128)(2,1)} %bitcast.36, f32[1536,1]{1,0:T(8,128)} %copy.27.scale_ref), custom_call_target="tpu_custom_call" | custom-call | flops 14495514624 | bytes 23068672 | tf_op jit(solution)/shard_map/channel/pallas_call | solution.py:437
  194.0 104.6 %all_to_all.10.back_ref = bf16[128,256,128]{2,1,0:T(8,128)(2,1)} all-to-all(bf16[128,256,128]{2,1,0:T(8,128)(2,1)} %channel.1), channel_id=1, replica_groups=mesh['row'=8,'col'=16] {'col','row'}, dimensions={0} | all-to-all | bytes 16777216 | tf_op jit(solution)/shard_map/all_to_all | solution.py:391
  298.6 6.2 %update.1 = bf16[1536,768]{1,0:T(8,128)(2,1)} custom-call(s32[256]{0:T(256)} %get-tuple-element.9.tile_ref, f32[256]{0:T(256)} %get-tuple-element.10.factor_ref, bf16[128,256,128]{2,1,0:T(8,128)(2,1)} %all_to_all.10.back_ref), custom_call_target="tpu_custom_call" | custom-call | bytes 11534336 | tf_op jit(solution)/shard_map/update/pallas_call | solution.py:463
  304.8 2.6 reduce-scatter.2.cloned.1.call-done.in_ref
  307.4 1.9 turn.1
  (1 shorter events, 0.0 us)
Async XLA Ops:
  7.2 10.7 %copy-start.1 = (bf16[1,144]{1,0:T(2,128)(2,1)S(1)}, bf16[1,144]{1,0:T(2,128)(2,1)}, u32[]{:S(2)}) copy-start(bf16[1,144]{1,0:T(2,128)(2,1)} %param.22) | copy-start | bytes 868
  7.2 117.6 %all-gather.2.cloned.1.call-start = ((), (), s32[]{:S(2)}) async-start(), calls=%async_computation.3 | async-start | bytes 7077888 | tf_op jit(solution)/shard_map/all_gather | solution.py:358
  10.0 17.6 %collective-permute-start = (bf16[2,768,128]{2,1,0:T(8,128)(2,1)S(1)}, bf16[2,768,128]{2,1,0:T(8,128)(2,1)S(1)}, u32[]{:S(2)}, u32[]{:S(2)}) collective-permute-start(bf16[2,768,128]{2,1,0:T(8,128)(2,1)S(1)} %fusion.2), channel_id=1, source_target_pairs={{0,65},{1,0},{2,81},{3,16},{4,97},{5,32},{6,113},{7,48},{8,1},{9,6... | collective-permute-start | bytes 1179656 | tf_op jit(solution)/shard_map/ppermute | solution.py:353
  14.1 15.4 %collective-permute-start.1 = (bf16[2,768,128]{2,1,0:T(8,128)(2,1)S(1)}, bf16[2,768,128]{2,1,0:T(8,128)(2,1)S(1)}, u32[]{:S(2)}, u32[]{:S(2)}) collective-permute-start(bf16[2,768,128]{2,1,0:T(8,128)(2,1)S(1)} %fusion), channel_id=1, source_target_pairs={{0,0},{1,65},{2,16},{3,81},{4,32},{5,97},{6,48},{7,113},{8,64},{9,... | collective-permute-start | bytes 1179656 | tf_op jit(solution)/shard_map/ppermute | solution.py:352
  30.5 136.9 %all-to-all-start = ((bf16[128,264,128]{2,1,0:T(8,128)(2,1)}), bf16[128,264,128]{2,1,0:T(8,128)(2,1)}, u32[]{:S(2)}, u32[]{:S(2)}) async-start(bf16[128,264,128]{2,1,0:T(8,128)(2,1)} %get-tuple-element.11), calls=%async_computation.1 | async-start | bytes 17301504 | tf_op jit(solution)/shard_map/all_to_all | solution.py:391
  41.5 266.0 %reduce-scatter.2.cloned.1.call-start = ((), (), s32[]{:S(2)}) async-start(), calls=%async_computation.4 | async-start | bytes 6684672 | tf_op jit(solution)/shard_map/reduce_scatter | solution.py:385
  140.7 0.7 copy-start
Sparse Core Ops, SparseCore 0:
  30.6 94.0 all-gather.1
  140.8 166.5 reduce-scatter.1
